TPU v7x, 512 devices: a whole 4x8x8 slice. The times are simulated.
512 devices in a mesh: dp: 16 (over z, core), expert: 8 (over y), tensor: 4 (over x).
Axes of the slice: x: 4, y: 8, z: 8, core: 2. Of those that a mesh axis runs over, the one named last changes fastest.
Arguments:
- expert_out: bfloat16 [8, 24576, 3072], P('expert', 'dp', 'tensor'), parts along dimension 1, may hold values from -6 to 6
- kept_blocks: int32 [8, 192], P('expert', 'dp'), parts along dimension 1, may hold values from 0 to 1, as said below
- expert_ids: int32 [65536, 2], P(('dp', 'expert', 'tensor')), parts along dimension 0, may hold values from 0 to 7, all different within a row; in each aligned block of 128 rows (0 to 127, 128 to 255, ...) at most 48 rows name the same one
- gate_levels: int32 [65536, 2], P(('dp', 'expert', 'tensor')), parts along dimension 0, may hold values from 16 to 240
- norm_gain: bfloat16 [3072], replicated, may hold values from 0.099609375 to 1.8984375
- qkv_weight: bfloat16 [3072, 4096], P('expert', 'tensor'), may hold values from -0.109375 to 0.109375
Outputs:
- qkv: bfloat16 [65536, 4096], P(('dp', 'expert'), 'tensor'), parts along dimension 0
There are 16 independent parts, one for each index of `dp`. A program takes and returns all parts, laid end to end along the dimension named above; an argument that names none is the same for every part. Nothing has to cross between parts.
Inputs may be any that keep to these rules, and one draw needn't show every extreme that they name: `kept_blocks`: each expert keeps a leading run of one or more of its 12 blocks; in every draw some expert keeps all of them. `expert_ids`: the two experts of a token differ; among the tokens of one owner device (aligned blocks of 128 rows) each expert is named at most 48 times, a bound that some block reaches.
All inputs are finite; a program needn't handle non-finite values.
Results may differ from a plain program's by a relative error of at most 0.0049.
Values may be sent and summed in bfloat16 or wider, within the bound.
No kernel may reach another device: no remote copies, remote signals or barrier semaphores. Data moves between devices by JAX's collectives and lax.ppermute only.
A program may use at most 64 MiB of HBM per device.

v0:
```python
import jax
import jax.numpy as jnp
from jax import lax
from jax.sharding import PartitionSpec as P


def local(expert_out, kept_blocks, expert_ids, gate_levels, norm_gain, qkv_weight):
    expert_size = lax.axis_size("expert")
    tensor_size = lax.axis_size("tensor")
    devices = expert_size * tensor_size
    row_total = expert_out.shape[1]
    quarter = expert_out.shape[2]
    slot_total = row_total // devices
    block_rows = 4 * devices
    row_mask = jnp.repeat(kept_blocks[0], block_rows).astype(jnp.bfloat16)
    outputs = expert_out[0] * row_mask[:, None]
    outgoing = outputs.reshape(slot_total, devices, quarter)
    incoming = lax.all_to_all(
        outgoing, ("expert", "tensor"), split_axis=1, concat_axis=1, tiled=True
    )
    arrived = incoming.reshape(slot_total * expert_size, tensor_size * quarter)
    one_hot = (expert_ids[:, :, None] == jnp.arange(expert_size)[None, None, :]).astype(jnp.int32)
    per_token = jnp.sum(one_hot, axis=1)
    earlier = jnp.cumsum(per_token, axis=0) - per_token
    slot_rank = jnp.sum(earlier[:, None, :] * one_hot, axis=-1)
    row_index = slot_rank * expert_size + expert_ids
    tok_count = expert_ids.shape[0]
    picked = (
        jnp.take(arrived, row_index.reshape(-1), axis=0)
        .reshape(tok_count, 2, -1)
        .astype(jnp.float32)
    )
    gate_share = gate_levels.astype(jnp.float32) / 256.0
    combined = jnp.sum(gate_share[:, :, None] * picked, axis=1)
    scale = lax.rsqrt(jnp.mean(combined * combined, axis=-1, keepdims=True) + 1e-05)
    normed = (combined * scale * norm_gain.astype(jnp.float32)).astype(jnp.bfloat16)
    group = lax.all_gather(normed, "tensor", axis=0, tiled=True)
    projected = jnp.dot(
        group,
        lax.all_gather(qkv_weight, "expert", axis=0, tiled=True),
        preferred_element_type=jnp.float32,
    )
    return projected.astype(jnp.bfloat16)


def solution(mesh):
    in_specs = (
        P("expert", "dp", "tensor"),
        P("expert", "dp"),
        P(("dp", "expert", "tensor"), None),
        P(("dp", "expert", "tensor"), None),
        P(),
        P("expert", "tensor"),
    )
    out_specs = P(("dp", "expert"), "tensor")
    return jax.shard_map(local, mesh=mesh, in_specs=in_specs, out_specs=out_specs, check_vma=False)
```

profile of v0, /device:TPU:1, one launch (start us, length us, event | category | flops | bytes accessed | tf_op | source)
XLA Modules:
  0.0 238.4 jit_solution(11101187993803095623)
XLA Ops:
  6.5 0.7 convert_bitcast_fusion
  7.2 0.1 broadcast_in_dim.13
  7.3 0.1 convert_element_type.37
  7.4 1.9 broadcast_multiply_fusion
  9.3 2.7 %copy.30 = bf16[48,32,768]{2,0,1:T(8,128)(2,1)} copy(bf16[48,32,768]{2,1,0:T(8,128)(2,1)S(1)} %broadcast_multiply_fusion) | data formatting | bytes 4718592 | tf_op jit(solution)/shard_map/mul | solution.py:16
  12.0 0.0 copy-start
  12.0 0.0 copy-start.2
  12.0 0.0 copy-start.1
  12.0 10.6 %all-to-all-start = ((bf16[48,32,768]{2,0,1:T(8,128)(2,1)}), bf16[48,32,768]{2,0,1:T(8,128)(2,1)S(1)}, u32[]{:S(2)}, u32[]{:S(2)}) async-start(bf16[48,32,768]{2,0,1:T(8,128)(2,1)} %copy.30), calls=%async_computation | async-start | bytes 4718592 | tf_op jit(solution)/shard_map/all_to_all | solution.py:18
  22.6 0.0 all-gather.3.cloned.1.call-start
  22.7 0.0 copy-done
  22.7 0.1 copy.26
  22.8 0.2 reduce_window_sum.11
  23.1 0.1 copy.32
  23.2 0.1 reshape.83
  23.3 0.1 copy.29
  23.5 0.0 copy-done.2
  23.5 0.1 copy.25
  23.6 0.0 copy-done.1
  23.6 52.9 %all-to-all-done = bf16[48,32,768]{2,0,1:T(8,128)(2,1)S(1)} async-done(((bf16[48,32,768]{2,0,1:T(8,128)(2,1)}), bf16[48,32,768]{2,0,1:T(8,128)(2,1)S(1)}, u32[]{:S(2)}, u32[]{:S(2)}) %all-to-all-start) | async-done | bytes 2359328 | tf_op jit(solution)/shard_map/all_to_all | solution.py:18
  76.5 2.1 copy.31
  78.7 3.9 %reshape.82 = bf16[384,3072]{1,0:T(8,128)(2,1)S(1)} reshape(bf16[48,32,768]{2,1,0:T(8,128)(2,1)} %copy.31) | data formatting | bytes 4718592 | tf_op jit(solution)/shard_map/reshape | solution.py:21
  82.5 2.7 %gather_fusion = bf16[256,3072]{1,0:T(8,128)(2,1)} fusion(bf16[384,3072]{1,0:T(8,128)(2,1)S(1)} %reshape.82, s32[1024]{0:T(1024)S(1)} %pad_clamp_fusion), kind=kCustom, calls=%fused_computation | custom fusion | bytes 3146752 | tf_op jit(solution)/shard_map/jit(_take)/gather | solution.py:29
  85.2 3.5 %gather.7 = bf16[128,2,3072]{2,1,0:T(2,128)(2,1)S(1)} reshape(bf16[256,3072]{1,0:T(8,128)(2,1)} %gather_fusion) | data formatting | bytes 3145728 | tf_op jit(solution)/shard_map/jit(_take)/gather | solution.py:29
  88.7 6.4 %multiply_reduce_fusion = f32[128,3072]{1,0:T(8,128)S(1)} fusion(bf16[128,2,3072]{2,1,0:T(2,128)(2,1)S(1)} %gather.7, pred[128,2]{1,0:T(8,128)(4,1)S(1)} %copy.29, f32[128,2]{1,0:T(8,128)S(1)} %copy.25), kind=kLoop, calls=%fused_computation.1 | loop fusion | flops 2752512 | bytes 3147008 | tf_op jit(solution)/shard_map/reduce_sum | solution.py:34
  95.2 0.2 multiply_reduce_fusion.1
  95.4 1.1 multiply_convert_fusion
  96.5 0.0 all-gather.3.cloned.1.call-update
  96.5 0.2 all-gather.5.cloned.1.call-start
  96.7 0.5 all-gather.5.cloned.1.call-update
  97.2 47.1 %all-gather.3.cloned.1.call-done = bf16[512,3072]{1,0:T(8,128)(2,1)} async-done(((bf16[128,3072]{1,0:T(8,128)(2,1)}), bf16[512,3072]{1,0:T(8,128)(2,1)}) %all-gather.3.cloned.1.call-update) | async-done | bytes 3145744 | tf_op jit(solution)/shard_map/all_gather | solution.py:37
  144.3 79.2 %all-gather.5.cloned.1.call-done = bf16[3072,1024]{1,0:T(8,128)(2,1)} async-done(((bf16[384,1024]{1,0:T(8,128)(2,1)}), bf16[3072,1024]{1,0:T(8,128)(2,1)}) %all-gather.5.cloned.1.call-update) | async-done | bytes 6291472 | tf_op jit(solution)/shard_map/all_gather | solution.py:40
  223.5 8.1 %convolution_convert_fusion = bf16[512,1024]{1,0:T(8,128)(2,1)} fusion(bf16[512,3072]{1,0:T(8,128)(2,1)} %all-gather.3.cloned.1.call-done, bf16[3072,1024]{1,0:T(8,128)(2,1)} %all-gather.5.cloned.1.call-done), kind=kOutput, calls=%fused_computation.5 | convolution fusion | flops 3221749760 | bytes 10485760 | tf_op jit(solution)/shard_map/dot_general | solution.py:38
  (10 shorter events, 0.1 us)
Async XLA Ops:
  12.0 10.7 %copy-start = (s32[128,2]{0,1:T(2,128)S(1)}, s32[128,2]{0,1:T(2,128)}, u32[]{:S(2)}) copy-start(s32[128,2]{0,1:T(2,128)} %param.8) | copy-start | bytes 3076
  12.0 11.5 %copy-start.2 = (s32[128,2]{0,1:T(2,128)S(1)}, s32[128,2]{0,1:T(2,128)}, u32[]{:S(2)}) copy-start(s32[128,2]{0,1:T(2,128)} %param.9) | copy-start | bytes 3076
  12.0 11.6 %copy-start.1 = (bf16[3072]{0:T(1024)(128)(2,1)S(1)}, bf16[3072]{0:T(1024)(128)(2,1)}, u32[]{:S(2)}) copy-start(bf16[3072]{0:T(1024)(128)(2,1)} %param.10) | copy-start | bytes 18436
  12.0 64.5 %all-to-all-start = ((bf16[48,32,768]{2,0,1:T(8,128)(2,1)}), bf16[48,32,768]{2,0,1:T(8,128)(2,1)S(1)}, u32[]{:S(2)}, u32[]{:S(2)}) async-start(bf16[48,32,768]{2,0,1:T(8,128)(2,1)} %copy.30), calls=%async_computation | async-start | bytes 4718592 | tf_op jit(solution)/shard_map/all_to_all | solution.py:18
  22.6 121.7 %all-gather.3.cloned.1.call-start = ((), (), s32[]{:S(2)}) async-start(), calls=%async_computation.1 | async-start | bytes 3932160 | tf_op jit(solution)/shard_map/all_gather | solution.py:37
  96.5 127.0 %all-gather.5.cloned.1.call-start = ((), (), s32[]{:S(2)}) async-start(), calls=%async_computation.2 | async-start | bytes 7077888 | tf_op jit(solution)/shard_map/all_gather | solution.py:40
Sparse Core Ops, SparseCore 0:
  96.6 47.6 all-gather.2
  146.4 77.0 all-gather.4
where the time goes:
time: 239 us; the launch traced here: 238 us
  waiting for transfers between devices  180 us (75%)
  local copies, waits for them, and re-layouts  15.8 us (7%)
  between operations  13.5 us (6%)
  starting transfers between devices  10.9 us (5%)
  other arithmetic  10.5 us (4%)
  matrix products  8.12 us (3%)
    all_gather x1, waiting for transfers between devices, local(): lax.all_gather(qkv_weight, 'expert', axis=0, tiled=True)  79.2 us
    all_to_all x1, waiting for transfers between devices, local(): lax.all_to_all(outgoing, ('expert', 'tensor'), split_axis=1, concat_axis=...  52.9 us
    all_gather x1, waiting for transfers between devices, local(): group = lax.all_gather(normed, 'tensor', axis=0, tiled=True)  47.1 us
    all_to_all x1, starting transfers between devices, local(): lax.all_to_all(outgoing, ('expert', 'tensor'), split_axis=1, concat_axis=...  10.6 us
    dot_general x1, matrix products, local(): jnp.dot(group, lax.all_gather(qkv_weight, 'expert', axis=0, tiled=True),...  8.12 us
    reduce_sum x1, other arithmetic, local(): combined = jnp.sum(gate_share[:, :, None] * picked, axis=1)  6.41 us
    gather x2, local copies, waits for them, and re-layouts, local(): jnp.take(arrived, row_index.reshape(-1), axis=0).reshape(tok_count, 2, -1)  6.21 us
  transfers between devices with their start and end apart: 3, of which 3 were waited for; matrix products, arithmetic and copies ran while one was open for 0% of the time, Pallas kernels for 0%

commit v1 on v0

v1 whole, which is shorter than its diff:
```python
import functools

import jax
import jax.numpy as jnp
from jax import lax
from jax.experimental import pallas as pl
from jax.experimental.pallas import tpu as pltpu
from jax.sharding import PartitionSpec as P

F32 = jnp.float32
BF16 = jnp.bfloat16
VMEM_LIMIT = 48 * 1024 * 1024


def select_kernel(experts, slots, ids_ref, sel_ref):
    tok = ids_ref.shape[1]
    cols = experts * slots
    row = lax.broadcasted_iota(jnp.int32, (tok, tok), 0)
    col = lax.broadcasted_iota(jnp.int32, (tok, tok), 1)
    before = (col < row).astype(F32).astype(BF16)
    lane = lax.broadcasted_iota(jnp.int32, (tok, 128), 1)
    place = lax.broadcasted_iota(jnp.int32, (tok, cols), 1)
    for q in range(ids_ref.shape[0]):
        both = ids_ref[q]
        hot = [(lane == both[:, k : k + 1]).astype(F32) for k in range(2)]
        earlier = jnp.dot(before, (hot[0] + hot[1]).astype(BF16), preferred_element_type=F32)
        total = jnp.zeros((tok, cols), F32)
        for k in range(2):
            slot = jnp.sum(earlier * hot[k], axis=1, keepdims=True).astype(jnp.int32)
            target = both[:, k : k + 1] * slots + slot
            share = both[:, 2 + k : 3 + k].astype(F32) / 256.0
            total = total + jnp.where(place == target, share, 0.0)
        sel_ref[q] = total.astype(BF16)


def select(ids, experts, slots):
    owners, tok, _ = ids.shape
    return pl.pallas_call(
        functools.partial(select_kernel, experts, slots),
        out_shape=jax.ShapeDtypeStruct((owners, tok, experts * slots), BF16),
    )(ids)


def combine_kernel(sel_ref, rows_ref, gain_ref, out_ref):
    experts, owners, slots, width = rows_ref.shape
    tok = sel_ref.shape[1]
    for q in range(owners):
        rows = rows_ref[:, q].reshape(experts * slots, width)
        total = jnp.dot(sel_ref[q], rows, preferred_element_type=F32)
        out_ref[pl.ds(q * tok, tok), :] = (total * gain_ref[...]).astype(BF16)


def combine(sel, rows, gain):
    owners, tok, _ = sel.shape
    return pl.pallas_call(
        combine_kernel,
        out_shape=jax.ShapeDtypeStruct((owners * tok, rows.shape[3]), BF16),
    )(sel, rows, gain)


def project_kernel(width, place_ref, own_ref, one_ref, two_ref, three_ref, w_ref, inv_ref, *rest):
    out_ref, scale_ref = rest[-2:]
    blocks = (own_ref, one_ref, two_ref, three_ref)

    @pl.when(pl.program_id(0) == 0)
    def _():
        total = jnp.zeros(scale_ref.shape, F32)
        for k, block in enumerate(blocks):
            plain = block[...].astype(F32) * inv_ref[place_ref[k]]
            total = total + jnp.sum(plain * plain, axis=1, keepdims=True)
        scale_ref[...] = lax.rsqrt(total / width + 1e-05)

    acc = jnp.dot(own_ref[...], w_ref[place_ref[0]], preferred_element_type=F32)
    for k in range(1, 4):
        acc = acc + jnp.dot(blocks[k][...], w_ref[place_ref[k]], preferred_element_type=F32)
    out_ref[...] = (acc * scale_ref[...]).astype(BF16)


def project(place, blocks, weight, inv_gain, total_rows, row_block, into=None):
    rows, quarter = blocks[0].shape
    parts, _, columns = weight.shape
    tile = 256
    whole = pl.BlockSpec((rows, quarter), lambda j, p: (0, 0))
    in_specs = [whole] * 4 + [
        pl.BlockSpec((parts, quarter, tile), lambda j, p: (0, 0, j)),
        pl.BlockSpec((parts, 1, quarter), lambda j, p: (0, 0, 0)),
    ]
    args = [place, *blocks, weight, inv_gain]
    aliases = {}
    if into is not None:
        in_specs.append(pl.BlockSpec(memory_space=pl.ANY))
        aliases = {len(args): 0}
        args.append(into)
    return pl.pallas_call(
        functools.partial(project_kernel, parts * quarter),
        out_shape=jax.ShapeDtypeStruct((total_rows, columns), BF16),
        grid_spec=pltpu.PrefetchScalarGridSpec(
            num_scalar_prefetch=1,
            grid=(columns // tile,),
            in_specs=in_specs,
            out_specs=pl.BlockSpec((rows, tile), lambda j, p: (row_block, j)),
            scratch_shapes=[pltpu.VMEM((rows, 1), F32)],
        ),
        input_output_aliases=aliases,
        compiler_params=pltpu.CompilerParams(vmem_limit_bytes=VMEM_LIMIT),
    )(*args)


def local(expert_out, kept_blocks, expert_ids, gate_levels, norm_gain, qkv_weight):
    parts = lax.axis_size("dp")
    experts = lax.axis_size("expert")
    tensors = lax.axis_size("tensor")
    part, mine, quarter_of = (lax.axis_index(a) for a in ("dp", "expert", "tensor"))
    devices = experts * tensors
    rows, quarter = expert_out.shape[1:]
    slots = rows // devices
    tok = expert_ids.shape[0]

    share = qkv_weight.shape[0] // parts
    columns = qkv_weight.shape[1]
    w = lax.dynamic_slice(qkv_weight, (part * share, 0), (share, columns))
    w = w.reshape(1, 1, 1, share, columns)
    for axis, step in enumerate((4, 2, 1)):
        other = lax.ppermute(w, "expert", [(i, i ^ step) for i in range(experts)])
        upper = (mine & step) != 0
        w = jnp.concatenate([jnp.where(upper, other, w), jnp.where(upper, w, other)], axis=axis)
    w = lax.all_gather(w.reshape(experts * share, columns), "dp", axis=0, tiled=True)
    weight = (
        w.reshape(parts, experts, share, columns)
        .transpose(1, 0, 2, 3)
        .reshape(tensors, quarter, columns)
    )

    mask = jnp.repeat(kept_blocks[0], 4 * devices).astype(BF16)
    masked = (expert_out[0] * mask[:, None]).reshape(slots, experts, tensors, quarter)
    outgoing = masked.transpose(1, 2, 0, 3)

    ids = lax.all_gather(jnp.concatenate([expert_ids, gate_levels], axis=1), "tensor")
    sel = select(ids, experts, slots)

    gain = norm_gain.astype(F32)
    inv_gain = (1.0 / gain).reshape(tensors, 1, quarter)
    own_gain = lax.dynamic_slice(gain, (quarter_of * quarter,), (quarter,)).reshape(1, quarter)
    place = (quarter_of - jnp.arange(tensors, dtype=jnp.int32)) % tensors

    out = None
    for lo, hi in ((0, 3), (3, 4)):
        arrived = lax.all_to_all(outgoing[:, lo:hi], "expert", 0, 0, tiled=True)
        own = combine(sel[lo:hi], arrived, own_gain)
        blocks = [own] + [
            lax.ppermute(own, "tensor", [(i, (i + k) % tensors) for i in range(tensors)])
            for k in range(1, tensors)
        ]
        out = project(place, blocks, weight, inv_gain, tensors * tok, lo // (hi - lo), out)
    return out


def solution(mesh):
    in_specs = (
        P("expert", "dp", "tensor"),
        P("expert", "dp"),
        P(("dp", "expert", "tensor"), None),
        P(("dp", "expert", "tensor"), None),
        P(),
        P("expert", "tensor"),
    )
    out_specs = P(("dp", "expert"), "tensor")
    return jax.shard_map(local, mesh=mesh, in_specs=in_specs, out_specs=out_specs, check_vma=False)
```

time: 239 us -> 176 us (0.74)
  the two profiles are of different devices: /device:TPU:1 before, /device:TPU:10 now
where the time goes in v1:
time: 176 us; the launch traced here: 175 us
  starting transfers between devices  54.3 us (31%)
  waiting for transfers between devices  51.3 us (29%)
  Pallas kernels  21.5 us (12%)
  local copies, waits for them, and re-layouts  17.7 us (10%)
  between operations  13.6 us (8%)
  blocking collectives  10.8 us (6%)
  other arithmetic  5.98 us (3%)
    all_to_all x2, waiting for transfers between devices, local(): arrived = lax.all_to_all(outgoing[:, lo:hi], 'expert', 0, 0, tiled=True)  40 us
    ppermute x6, starting transfers between devices, local(): lax.ppermute(own, 'tensor', [(i, (i + k) % tensors) for i in range(tensor...  26.5 us
    ppermute x3, starting transfers between devices, local(): other = lax.ppermute(w, 'expert', [(i, i ^ step) for i in range(experts)])  15.3 us
    pallas_call x2, Pallas kernels, project(): pl.pallas_call(functools.partial(project_kernel, parts * quarter), out_sh...  13.1 us
    all_to_all x2, starting transfers between devices, local(): arrived = lax.all_to_all(outgoing[:, lo:hi], 'expert', 0, 0, tiled=True)  12.5 us
    ppermute x3, waiting for transfers between devices, local(): other = lax.ppermute(w, 'expert', [(i, i ^ step) for i in range(experts)])  11.3 us
    all_gather x1, blocking collectives, local(): lax.all_gather(jnp.concatenate([expert_ids, gate_levels], axis=1), 'tensor')  10.8 us
    transpose x1, local copies, waits for them, and re-layouts, local(): weight = w.reshape(parts, experts, share, columns).transpose(1, 0, 2, 3)....  6.47 us
  transfers between devices with their start and end apart: 12, of which 4 were waited for; matrix products, arithmetic and copies ran while one was open for 12% of the time, Pallas kernels for 9%

profile of v1, /device:TPU:10, one launch (start us, length us, event | category | flops | bytes accessed | tf_op | source)
XLA Modules:
  0.0 175.2 jit_solution(114757567776334241)
XLA Ops:
  6.5 0.0 copy-start.2
  6.5 0.0 all-gather.3.cloned.1.call-start
  6.5 1.0 dynamic-slice_bitcast_fusion
  7.5 6.8 %collective-permute-start.3 = (bf16[1,1,1,24,1024]{4,3,2,1,0:T(8,128)(2,1)S(1)}, bf16[1,1,1,24,1024]{4,3,2,1,0:T(8,128)(2,1)S(1)}, u32[]{:S(2)}, u32[]{:S(2)}) collective-permute-start(bf16[1,1,1,24,1024]{4,3,2,1,0:T(8,128)(2,1)S(1)} %dynamic-slice_bitcast_fusion), channel_id=1, source_target_pairs={{0,16},{4,20},{8,24},{12,28},{16,0},{20,4},{24,8},{28,12},{1,17},{... | collective-permute-start | bytes 147464 | tf_op jit(solution)/shard_map/ppermute | solution.py:124
  14.3 3.1 %collective-permute-done.3 = bf16[1,1,1,24,1024]{4,3,2,1,0:T(8,128)(2,1)S(1)} collective-permute-done((bf16[1,1,1,24,1024]{4,3,2,1,0:T(8,128)(2,1)S(1)}, bf16[1,1,1,24,1024]{4,3,2,1,0:T(8,128)(2,1)S(1)}, u32[]{:S(2)}, u32[]{:S(2)}) %collective-permute-start.3) | collective-permute-done | bytes 49184 | tf_op jit(solution)/shard_map/ppermute | solution.py:124
  17.5 0.8 broadcast_select_fusion.5
  18.3 4.4 %collective-permute-start.4 = (bf16[2,1,1,24,1024]{4,3,2,1,0:T(8,128)(2,1)S(1)}, bf16[2,1,1,24,1024]{4,3,2,1,0:T(8,128)(2,1)S(1)}, u32[]{:S(2)}, u32[]{:S(2)}) collective-permute-start(bf16[2,1,1,24,1024]{4,3,2,1,0:T(8,128)(2,1)S(1)} %pad_maximum_fusion.2), channel_id=1, source_target_pairs={{0,8},{4,12},{8,0},{12,4},{16,24},{20,28},{24,16},{28,20},{1,9},{5... | collective-permute-start | bytes 294920 | tf_op jit(solution)/shard_map/ppermute | solution.py:124
  22.7 3.2 %collective-permute-done.4 = bf16[2,1,1,24,1024]{4,3,2,1,0:T(8,128)(2,1)S(1)} collective-permute-done((bf16[2,1,1,24,1024]{4,3,2,1,0:T(8,128)(2,1)S(1)}, bf16[2,1,1,24,1024]{4,3,2,1,0:T(8,128)(2,1)S(1)}, u32[]{:S(2)}, u32[]{:S(2)}) %collective-permute-start.4) | collective-permute-done | bytes 98336 | tf_op jit(solution)/shard_map/ppermute | solution.py:124
  26.0 4.0 %collective-permute-start.5 = (bf16[2,2,1,24,1024]{4,3,2,1,0:T(8,128)(2,1)S(1)}, bf16[2,2,1,24,1024]{4,3,2,1,0:T(8,128)(2,1)S(1)}, u32[]{:S(2)}, u32[]{:S(2)}) collective-permute-start(bf16[2,2,1,24,1024]{4,3,2,1,0:T(8,128)(2,1)S(1)} %pad_maximum_fusion.1), channel_id=1, source_target_pairs={{0,4},{4,0},{8,12},{12,8},{16,20},{20,16},{24,28},{28,24},{1,5},{5... | collective-permute-start | bytes 589832 | tf_op jit(solution)/shard_map/ppermute | solution.py:124
  30.0 4.9 %collective-permute-done.5 = bf16[2,2,1,24,1024]{4,3,2,1,0:T(8,128)(2,1)S(1)} collective-permute-done((bf16[2,2,1,24,1024]{4,3,2,1,0:T(8,128)(2,1)S(1)}, bf16[2,2,1,24,1024]{4,3,2,1,0:T(8,128)(2,1)S(1)}, u32[]{:S(2)}, u32[]{:S(2)}) %collective-permute-start.5) | collective-permute-done | bytes 196640 | tf_op jit(solution)/shard_map/ppermute | solution.py:124
  35.0 0.8 pad_maximum_fusion
  35.8 0.0 all-gather.3.cloned.1.call-update
  35.8 0.0 copy-done.2
  35.8 0.0 copy-start.7
  35.9 2.3 %squeeze.4 = bf16[48,8,4,768]{3,2,1,0:T(4,128)(2,1)} reshape(bf16[1,1536,768]{2,1,0:T(8,128)(2,1)S(1)} %copy-done.2) | data formatting | bytes 4718592 | tf_op jit(solution)/shard_map/squeeze | solution.py:135
  38.1 0.0 copy-done.7
  38.1 0.1 broadcast_in_dim.4
  38.2 0.1 convert_element_type.20
  38.3 4.3 %fusion = bf16[8,4,48,768]{3,2,1,0:T(8,128)(2,1)S(1)} fusion(bf16[48,8,4,768]{3,2,1,0:T(4,128)(2,1)} %squeeze.4, bf16[48]{0:T(256)(128)(2,1)S(1)} %convert_element_type.20), kind=kLoop, calls=%fused_computation.1 | loop fusion | flops 1179648 | bytes 4718688 | tf_op jit(solution)/shard_map/transpose | solution.py:136
  42.5 1.4 slice.19
  43.9 0.0 copy-start.4
  43.9 0.0 copy-start.5
  43.9 0.0 copy-start.6
  44.0 7.6 %all-to-all-start.1 = ((bf16[8,3,48,768]{3,2,1,0:T(8,128)(2,1)}), bf16[8,3,48,768]{3,2,1,0:T(8,128)(2,1)}, u32[]{:S(2)}, u32[]{:S(2)}) async-start(bf16[8,3,48,768]{3,2,1,0:T(8,128)(2,1)} %slice.19), calls=%async_computation.1 | async-start | bytes 3538944 | tf_op jit(solution)/shard_map/all_to_all | solution.py:148
  51.5 0.9 slice.17
  52.4 40.0 %all-to-all-done.1.rows_ref = bf16[8,3,48,768]{3,2,1,0:T(8,128)(2,1)} async-done(((bf16[8,3,48,768]{3,2,1,0:T(8,128)(2,1)}), bf16[8,3,48,768]{3,2,1,0:T(8,128)(2,1)}, u32[]{:S(2)}, u32[]{:S(2)}) %all-to-all-start.1) | async-done | bytes 1769504 | tf_op jit(solution)/shard_map/all_to_all | solution.py:148
  92.4 4.9 %all-to-all-start = ((bf16[8,1,48,768]{3,2,1,0:T(8,128)(2,1)}), bf16[8,1,48,768]{3,2,1,0:T(8,128)(2,1)S(1)}, u32[]{:S(2)}, u32[]{:S(2)}) async-start(bf16[8,1,48,768]{3,2,1,0:T(8,128)(2,1)} %slice.17), calls=%async_computation | async-start | bytes 1179648 | tf_op jit(solution)/shard_map/all_to_all | solution.py:148
  97.3 0.0 copy-done.4
  97.3 0.1 dynamic_slice.6
  97.4 0.6 reshape.34.gain_ref
  98.0 0.0 copy-done.5
  98.0 0.0 copy-done.6
  98.0 10.8 %all-gather = s32[512,4]{0,1:T(4,128)S(1)} all-gather(s32[128,4]{0,1:T(4,128)S(1)} %pad_add_fusion), channel_id=2, replica_groups=mesh['dp'=16,'expert'=8,'tensor'=4] {'tensor'}, dimensions={0}, use_global_device_ids=true | all-gather | bytes 10240 | tf_op jit(solution)/shard_map/all_gather | solution.py:138
  108.8 0.9 copy.9
  109.6 3.5 %shard_map.64 = bf16[4,128,384]{2,1,0:T(8,128)(2,1)} custom-call(s32[4,128,4]{2,1,0:T(8,128)} %bitcast.21), custom_call_target="tpu_custom_call" | custom-call | tf_op jit(solution)/shard_map/pallas_call | solution.py:38
  113.1 1.7 slice.18.sel_ref
  114.9 2.9 %shard_map.66.own_ref = bf16[384,768]{1,0:T(8,128)(2,1)} custom-call(bf16[3,128,384]{2,1,0:T(8,128)(2,1)} %slice.18.sel_ref, bf16[8,3,48,768]{3,2,1,0:T(8,128)(2,1)} %all-to-all-done.1.rows_ref, f32[1,768]{1,0:T(1,128)} %reshape.34.gain_ref), custom_call_target="tpu_custom_call" | custom-call | tf_op jit(solution)/shard_map/pallas_call | solution.py:55
  117.7 2.7 %collective-permute-start.6 = (bf16[384,768]{1,0:T(8,128)(2,1)}, bf16[384,768]{1,0:T(8,128)(2,1)S(1)}, u32[]{:S(2)}, u32[]{:S(2)}) collective-permute-start(bf16[384,768]{1,0:T(8,128)(2,1)} %shard_map.66.own_ref), channel_id=1, source_target_pairs={{0,1},{1,2},{2,3},{3,0},{4,5},{5,6},{6,7},{7,4},{8,9},{9,10},{10,1... | collective-permute-start | bytes 1769480 | tf_op jit(solution)/shard_map/ppermute | solution.py:151
  120.4 4.0 %collective-permute-start.7 = (bf16[384,768]{1,0:T(8,128)(2,1)}, bf16[384,768]{1,0:T(8,128)(2,1)S(1)}, u32[]{:S(2)}, u32[]{:S(2)}) collective-permute-start(bf16[384,768]{1,0:T(8,128)(2,1)} %shard_map.66.own_ref), channel_id=1, source_target_pairs={{0,2},{1,3},{2,0},{3,1},{4,6},{5,7},{6,4},{7,5},{8,10},{9,11},{10,... | collective-permute-start | bytes 1769480 | tf_op jit(solution)/shard_map/ppermute | solution.py:151
  124.4 3.1 %collective-permute-start.8 = (bf16[384,768]{1,0:T(8,128)(2,1)}, bf16[384,768]{1,0:T(8,128)(2,1)S(1)}, u32[]{:S(2)}, u32[]{:S(2)}) collective-permute-start(bf16[384,768]{1,0:T(8,128)(2,1)} %shard_map.66.own_ref), channel_id=1, source_target_pairs={{0,3},{1,0},{2,1},{3,2},{4,7},{5,4},{6,5},{7,6},{8,11},{9,8},{10,9... | collective-permute-start | bytes 1769480 | tf_op jit(solution)/shard_map/ppermute | solution.py:151
  127.5 1.6 slice.16.sel_ref
  129.1 0.0 all-to-all-done.rows_ref
  129.1 0.0 copy-start.3
  129.1 0.8 copy-done.3
  129.9 2.0 %shard_map.65.own_ref = bf16[128,768]{1,0:T(8,128)(2,1)} custom-call(bf16[1,128,384]{2,1,0:T(8,128)(2,1)} %slice.16.sel_ref, bf16[8,1,48,768]{3,2,1,0:T(8,128)(2,1)} %copy-done.3, f32[1,768]{1,0:T(1,128)} %reshape.34.gain_ref), custom_call_target="tpu_custom_call" | custom-call | tf_op jit(solution)/shard_map/pallas_call | solution.py:55
  131.9 2.7 %collective-permute-start = (bf16[128,768]{1,0:T(8,128)(2,1)}, bf16[128,768]{1,0:T(8,128)(2,1)S(1)}, u32[]{:S(2)}, u32[]{:S(2)}) collective-permute-start(bf16[128,768]{1,0:T(8,128)(2,1)} %shard_map.65.own_ref), channel_id=1, source_target_pairs={{0,1},{1,2},{2,3},{3,0},{4,5},{5,6},{6,7},{7,4},{8,9},{9,10},{10,1... | collective-permute-start | bytes 589832 | tf_op jit(solution)/shard_map/ppermute | solution.py:151
  134.7 4.6 %collective-permute-start.1 = (bf16[128,768]{1,0:T(8,128)(2,1)}, bf16[128,768]{1,0:T(8,128)(2,1)S(1)}, u32[]{:S(2)}, u32[]{:S(2)}) collective-permute-start(bf16[128,768]{1,0:T(8,128)(2,1)} %shard_map.65.own_ref), channel_id=1, source_target_pairs={{0,2},{1,3},{2,0},{3,1},{4,6},{5,7},{6,4},{7,5},{8,10},{9,11},{10,... | collective-permute-start | bytes 589832 | tf_op jit(solution)/shard_map/ppermute | solution.py:151
  139.3 0.0 collective-permute-done.6.one_ref
  139.3 9.4 %collective-permute-start.2 = (bf16[128,768]{1,0:T(8,128)(2,1)}, bf16[128,768]{1,0:T(8,128)(2,1)S(1)}, u32[]{:S(2)}, u32[]{:S(2)}) collective-permute-start(bf16[128,768]{1,0:T(8,128)(2,1)} %shard_map.65.own_ref), channel_id=1, source_target_pairs={{0,3},{1,0},{2,1},{3,2},{4,7},{5,4},{6,5},{7,6},{8,11},{9,8},{10,9... | collective-permute-start | bytes 589832 | tf_op jit(solution)/shard_map/ppermute | solution.py:151
  148.7 0.0 all-gather.3.cloned.1.call-done
  148.8 0.0 copy-start
  148.8 6.5 %copy.11 = bf16[8,16,24,1024]{3,2,1,0:T(8,128)(2,1)} copy(bf16[8,16,24,1024]{3,2,0,1:T(8,128)(2,1)} %bitcast.19) | data formatting | bytes 12582912 | tf_op jit(solution)/shard_map/transpose | solution.py:130
  155.2 0.0 collective-permute-done.7.two_ref
  155.2 0.0 collective-permute-done.8.three_ref
  155.2 0.0 copy-done
  155.3 0.0 copy-start.1
  155.3 7.3 %shard_map.67.rest_0_ = bf16[512,1024]{1,0:T(8,128)(2,1)} custom-call(s32[4]{0:T(128)S(1)} %and_select_fusion.place_ref, bf16[384,768]{1,0:T(8,128)(2,1)S(1)} %copy-done, bf16[384,768]{1,0:T(8,128)(2,1)S(1)} %collective-permute-done.6.one_ref, bf16[384,768]{1,0:T(8,128)(2,1)S(1)} %collective-permute-done.7.two_ref, ...), custom_call_target="tpu_custom_call" | custom-call | tf_op jit(solution)/shard_map/pallas_call | solution.py:94
  162.6 0.0 collective-permute-done.one_ref
  162.6 0.0 collective-permute-done.1.two_ref
  162.6 0.0 collective-permute-done.2.three_ref
  162.6 0.0 copy-done.1
  162.6 5.8 %shard_map.68 = bf16[512,1024]{1,0:T(8,128)(2,1)} custom-call(s32[4]{0:T(128)S(1)} %and_select_fusion.place_ref, bf16[128,768]{1,0:T(8,128)(2,1)S(1)} %copy-done.1, bf16[128,768]{1,0:T(8,128)(2,1)S(1)} %collective-permute-done.one_ref, bf16[128,768]{1,0:T(8,128)(2,1)S(1)} %collective-permute-done.1.two_ref, ...), custom_call_target="tpu_custom_call", output_to_operand_aliasing={{}: (7, {})} | custom-call | tf_op jit(solution)/shard_map/pallas_call | solution.py:94
  (8 shorter events, 0.1 us)
Async XLA Ops:
  6.5 29.3 %copy-start.2 = (bf16[1,1536,768]{2,1,0:T(8,128)(2,1)S(1)}, bf16[1,1536,768]{2,1,0:T(8,128)(2,1)}, u32[]{:S(2)}) copy-start(bf16[1,1536,768]{2,1,0:T(8,128)(2,1)} %param.6) | copy-start | bytes 7077892
  6.5 142.2 %all-gather.3.cloned.1.call-start = ((), (), s32[]{:S(2)}) async-start(), calls=%async_computation.2 | async-start | bytes 6684672 | tf_op jit(solution)/shard_map/all_gather | solution.py:127
  7.5 10.0 %collective-permute-start.3 = (bf16[1,1,1,24,1024]{4,3,2,1,0:T(8,128)(2,1)S(1)}, bf16[1,1,1,24,1024]{4,3,2,1,0:T(8,128)(2,1)S(1)}, u32[]{:S(2)}, u32[]{:S(2)}) collective-permute-start(bf16[1,1,1,24,1024]{4,3,2,1,0:T(8,128)(2,1)S(1)} %dynamic-slice_bitcast_fusion), channel_id=1, source_target_pairs={{0,16},{4,20},{8,24},{12,28},{16,0},{20,4},{24,8},{28,12},{1,17},{... | collective-permute-start | bytes 147464 | tf_op jit(solution)/shard_map/ppermute | solution.py:124
  18.3 7.6 %collective-permute-start.4 = (bf16[2,1,1,24,1024]{4,3,2,1,0:T(8,128)(2,1)S(1)}, bf16[2,1,1,24,1024]{4,3,2,1,0:T(8,128)(2,1)S(1)}, u32[]{:S(2)}, u32[]{:S(2)}) collective-permute-start(bf16[2,1,1,24,1024]{4,3,2,1,0:T(8,128)(2,1)S(1)} %pad_maximum_fusion.2), channel_id=1, source_target_pairs={{0,8},{4,12},{8,0},{12,4},{16,24},{20,28},{24,16},{28,20},{1,9},{5... | collective-permute-start | bytes 294920 | tf_op jit(solution)/shard_map/ppermute | solution.py:124
  26.0 9.0 %collective-permute-start.5 = (bf16[2,2,1,24,1024]{4,3,2,1,0:T(8,128)(2,1)S(1)}, bf16[2,2,1,24,1024]{4,3,2,1,0:T(8,128)(2,1)S(1)}, u32[]{:S(2)}, u32[]{:S(2)}) collective-permute-start(bf16[2,2,1,24,1024]{4,3,2,1,0:T(8,128)(2,1)S(1)} %pad_maximum_fusion.1), channel_id=1, source_target_pairs={{0,4},{4,0},{8,12},{12,8},{16,20},{20,16},{24,28},{28,24},{1,5},{5... | collective-permute-start | bytes 589832 | tf_op jit(solution)/shard_map/ppermute | solution.py:124
  35.8 2.3 %copy-start.7 = (s32[1,12]{1,0:T(1,128)S(1)}, s32[1,12]{1,0:T(1,128)}, u32[]{:S(2)}) copy-start(s32[1,12]{1,0:T(1,128)} %param.7) | copy-start | bytes 148
  43.9 53.3 %copy-start.4 = (bf16[3072]{0:T(1024)(128)(2,1)S(1)}, bf16[3072]{0:T(1024)(128)(2,1)}, u32[]{:S(2)}) copy-start(bf16[3072]{0:T(1024)(128)(2,1)} %param.10) | copy-start | bytes 18436
  43.9 54.0 %copy-start.5 = (s32[128,2]{0,1:T(2,128)S(1)}, s32[128,2]{0,1:T(2,128)}, u32[]{:S(2)}) copy-start(s32[128,2]{0,1:T(2,128)} %param.9) | copy-start | bytes 3076
  43.9 54.0 %copy-start.6 = (s32[128,2]{0,1:T(2,128)S(1)}, s32[128,2]{0,1:T(2,128)}, u32[]{:S(2)}) copy-start(s32[128,2]{0,1:T(2,128)} %param.8) | copy-start | bytes 3076
  44.0 48.4 %all-to-all-start.1 = ((bf16[8,3,48,768]{3,2,1,0:T(8,128)(2,1)}), bf16[8,3,48,768]{3,2,1,0:T(8,128)(2,1)}, u32[]{:S(2)}, u32[]{:S(2)}) async-start(bf16[8,3,48,768]{3,2,1,0:T(8,128)(2,1)} %slice.19), calls=%async_computation.1 | async-start | bytes 3538944 | tf_op jit(solution)/shard_map/all_to_all | solution.py:148
  92.4 36.8 %all-to-all-start = ((bf16[8,1,48,768]{3,2,1,0:T(8,128)(2,1)}), bf16[8,1,48,768]{3,2,1,0:T(8,128)(2,1)S(1)}, u32[]{:S(2)}, u32[]{:S(2)}) async-start(bf16[8,1,48,768]{3,2,1,0:T(8,128)(2,1)} %slice.17), calls=%async_computation | async-start | bytes 1179648 | tf_op jit(solution)/shard_map/all_to_all | solution.py:148
  117.7 21.6 %collective-permute-start.6 = (bf16[384,768]{1,0:T(8,128)(2,1)}, bf16[384,768]{1,0:T(8,128)(2,1)S(1)}, u32[]{:S(2)}, u32[]{:S(2)}) collective-permute-start(bf16[384,768]{1,0:T(8,128)(2,1)} %shard_map.66.own_ref), channel_id=1, source_target_pairs={{0,1},{1,2},{2,3},{3,0},{4,5},{5,6},{6,7},{7,4},{8,9},{9,10},{10,1... | collective-permute-start | bytes 1769480 | tf_op jit(solution)/shard_map/ppermute | solution.py:151
  120.4 34.8 %collective-permute-start.7 = (bf16[384,768]{1,0:T(8,128)(2,1)}, bf16[384,768]{1,0:T(8,128)(2,1)S(1)}, u32[]{:S(2)}, u32[]{:S(2)}) collective-permute-start(bf16[384,768]{1,0:T(8,128)(2,1)} %shard_map.66.own_ref), channel_id=1, source_target_pairs={{0,2},{1,3},{2,0},{3,1},{4,6},{5,7},{6,4},{7,5},{8,10},{9,11},{10,... | collective-permute-start | bytes 1769480 | tf_op jit(solution)/shard_map/ppermute | solution.py:151
  124.4 30.8 %collective-permute-start.8 = (bf16[384,768]{1,0:T(8,128)(2,1)}, bf16[384,768]{1,0:T(8,128)(2,1)S(1)}, u32[]{:S(2)}, u32[]{:S(2)}) collective-permute-start(bf16[384,768]{1,0:T(8,128)(2,1)} %shard_map.66.own_ref), channel_id=1, source_target_pairs={{0,3},{1,0},{2,1},{3,2},{4,7},{5,4},{6,5},{7,6},{8,11},{9,8},{10,9... | collective-permute-start | bytes 1769480 | tf_op jit(solution)/shard_map/ppermute | solution.py:151
  129.1 0.8 copy-start.3
  131.9 30.6 %collective-permute-start = (bf16[128,768]{1,0:T(8,128)(2,1)}, bf16[128,768]{1,0:T(8,128)(2,1)S(1)}, u32[]{:S(2)}, u32[]{:S(2)}) collective-permute-start(bf16[128,768]{1,0:T(8,128)(2,1)} %shard_map.65.own_ref), channel_id=1, source_target_pairs={{0,1},{1,2},{2,3},{3,0},{4,5},{5,6},{6,7},{7,4},{8,9},{9,10},{10,1... | collective-permute-start | bytes 589832 | tf_op jit(solution)/shard_map/ppermute | solution.py:151
  134.7 27.9 %collective-permute-start.1 = (bf16[128,768]{1,0:T(8,128)(2,1)}, bf16[128,768]{1,0:T(8,128)(2,1)S(1)}, u32[]{:S(2)}, u32[]{:S(2)}) collective-permute-start(bf16[128,768]{1,0:T(8,128)(2,1)} %shard_map.65.own_ref), channel_id=1, source_target_pairs={{0,2},{1,3},{2,0},{3,1},{4,6},{5,7},{6,4},{7,5},{8,10},{9,11},{10,... | collective-permute-start | bytes 589832 | tf_op jit(solution)/shard_map/ppermute | solution.py:151
  139.3 23.3 %collective-permute-start.2 = (bf16[128,768]{1,0:T(8,128)(2,1)}, bf16[128,768]{1,0:T(8,128)(2,1)S(1)}, u32[]{:S(2)}, u32[]{:S(2)}) collective-permute-start(bf16[128,768]{1,0:T(8,128)(2,1)} %shard_map.65.own_ref), channel_id=1, source_target_pairs={{0,3},{1,0},{2,1},{3,2},{4,7},{5,4},{6,5},{7,6},{8,11},{9,8},{10,9... | collective-permute-start | bytes 589832 | tf_op jit(solution)/shard_map/ppermute | solution.py:151
  148.8 6.5 %copy-start = (bf16[384,768]{1,0:T(8,128)(2,1)S(1)}, bf16[384,768]{1,0:T(8,128)(2,1)}, u32[]{:S(2)}) copy-start(bf16[384,768]{1,0:T(8,128)(2,1)} %shard_map.66.own_ref) | copy-start | bytes 1769476
  155.3 7.3 %copy-start.1 = (bf16[128,768]{1,0:T(8,128)(2,1)S(1)}, bf16[128,768]{1,0:T(8,128)(2,1)}, u32[]{:S(2)}) copy-start(bf16[128,768]{1,0:T(8,128)(2,1)} %shard_map.65.own_ref) | copy-start | bytes 589828
Sparse Core Ops, SparseCore 0:
  36.0 53.8 all-gather.2

commit v2 on v1

v2 whole, which is shorter than its diff:
```python
import functools

import jax
import jax.numpy as jnp
from jax import lax
from jax.experimental import pallas as pl
from jax.experimental.pallas import tpu as pltpu
from jax.sharding import PartitionSpec as P

F32 = jnp.float32
BF16 = jnp.bfloat16
VMEM_LIMIT = 48 * 1024 * 1024


def pack_kernel(kept_ref, rows_ref, *out_refs):
    slots, owners, width = rows_ref.shape
    per_block = 4
    step = pl.program_id(0)
    row = lax.broadcasted_iota(jnp.int32, (slots * owners, slots * owners), 0)
    col = lax.broadcasted_iota(jnp.int32, (slots * owners, slots * owners), 1)
    row_slot = lax.rem(row, slots)
    same = (lax.div(row, slots) == lax.rem(col, owners)) & (row_slot == lax.div(col, owners))
    block = lax.div(row_slot, per_block)
    kept = jnp.zeros(row.shape, jnp.int32)
    for b in range(slots // per_block):
        kept = jnp.where(block == b, kept_ref[step * (slots // per_block) + b], kept)
    move = (same & (kept != 0)).astype(F32).astype(BF16)
    moved = jnp.dot(
        move, rows_ref[...].reshape(slots * owners, width), preferred_element_type=F32
    ).astype(BF16)
    experts = out_refs[0].shape[0]
    moved = moved.reshape(experts, owners // experts, slots, width)
    at = 0
    for ref in out_refs:
        ref[...] = moved[:, at : at + ref.shape[1]]
        at += ref.shape[1]


def pack(kept, rows, experts, pieces):
    slots, owners, width = rows.shape
    step = 16
    return pl.pallas_call(
        pack_kernel,
        out_shape=[jax.ShapeDtypeStruct((experts, n, slots, width), BF16) for n in pieces],
        grid_spec=pltpu.PrefetchScalarGridSpec(
            num_scalar_prefetch=1,
            grid=(slots // step,),
            in_specs=[pl.BlockSpec((step, owners, width), lambda j, k: (j, 0, 0))],
            out_specs=[pl.BlockSpec((experts, n, step, width), lambda j, k: (0, 0, j, 0)) for n in pieces],
        ),
        compiler_params=pltpu.CompilerParams(vmem_limit_bytes=60 * 1024 * 1024),
    )(kept, rows)


def select_kernel(experts, slots, ids_ref, sel_ref):
    tok = ids_ref.shape[1]
    cols = experts * slots
    row = lax.broadcasted_iota(jnp.int32, (tok, tok), 0)
    col = lax.broadcasted_iota(jnp.int32, (tok, tok), 1)
    before = (col < row).astype(F32).astype(BF16)
    lane = lax.broadcasted_iota(jnp.int32, (tok, 128), 1)
    place = lax.broadcasted_iota(jnp.int32, (tok, cols), 1)
    for q in range(ids_ref.shape[0]):
        both = ids_ref[q]
        hot = [(lane == both[:, k : k + 1]).astype(F32) for k in range(2)]
        earlier = jnp.dot(before, (hot[0] + hot[1]).astype(BF16), preferred_element_type=F32)
        total = jnp.zeros((tok, cols), F32)
        for k in range(2):
            slot = jnp.sum(earlier * hot[k], axis=1, keepdims=True).astype(jnp.int32)
            target = both[:, k : k + 1] * slots + slot
            share = both[:, 2 + k : 3 + k].astype(F32) / 256.0
            total = total + jnp.where(place == target, share, 0.0)
        sel_ref[q] = total.astype(BF16)


def select(ids, experts, slots):
    owners, tok, _ = ids.shape
    return pl.pallas_call(
        functools.partial(select_kernel, experts, slots),
        out_shape=jax.ShapeDtypeStruct((owners, tok, experts * slots), BF16),
    )(ids)


def combine_kernel(sel_ref, rows_ref, gain_ref, out_ref):
    experts, owners, slots, width = rows_ref.shape
    tok = sel_ref.shape[1]
    for q in range(owners):
        rows = rows_ref[:, q].reshape(experts * slots, width)
        total = jnp.dot(sel_ref[q], rows, preferred_element_type=F32)
        out_ref[pl.ds(q * tok, tok), :] = (total * gain_ref[...]).astype(BF16)


def combine(sel, first, rows, gain):
    tok, cols = sel.shape[1:]
    experts, owners, slots, width = rows.shape
    return pl.pallas_call(
        combine_kernel,
        out_shape=jax.ShapeDtypeStruct((owners * tok, width), BF16),
        grid=(1,),
        in_specs=[
            pl.BlockSpec((owners, tok, cols), lambda i: (first // owners, 0, 0)),
            pl.BlockSpec(rows.shape, lambda i: (0, 0, 0, 0)),
            pl.BlockSpec(gain.shape, lambda i: (0, 0)),
        ],
        out_specs=pl.BlockSpec((owners * tok, width), lambda i: (0, 0)),
        cost_estimate=pl.CostEstimate(flops=45625000000, bytes_accessed=0, transcendentals=0),
        compiler_params=pltpu.CompilerParams(vmem_limit_bytes=VMEM_LIMIT),
    )(sel, rows, gain)


def project_kernel(width, pieces, place_ref, w_ref, inv_ref, *refs):
    blocks = [refs[4 * i : 4 * i + 4] for i in range(pieces)]
    out_ref, scale_ref = refs[-2:]
    half = pl.program_id(0)

    @pl.when(half == 0)
    def _():
        at = 0
        for piece in blocks:
            rows = piece[0].shape[0]
            total = jnp.zeros((rows, 1), F32)
            for k, block in enumerate(piece):
                plain = block[...].astype(F32) * inv_ref[place_ref[1 + k]]
                total = total + jnp.sum(plain * plain, axis=1, keepdims=True)
            scale_ref[pl.ds(at, rows), :] = lax.rsqrt(total / width + 1e-05)
            at += rows

    shards, _, share, _ = w_ref.shape
    at = 0
    for piece in blocks:
        rows = piece[0].shape[0]
        acc = None
        for k, block in enumerate(piece):
            for i in range(2):
                shard = 2 * place_ref[1 + k] + i
                plane = lax.rem(shard - place_ref[0] + 4 * half + shards, shards)
                term = jnp.dot(
                    block[:, i * share : (i + 1) * share], w_ref[plane, 0], preferred_element_type=F32
                )
                acc = term if acc is None else acc + term
        out_ref[pl.ds(at, rows), :] = (acc * scale_ref[pl.ds(at, rows), :]).astype(BF16)
        at += rows


def project(place, pieces, weight, inv_gain):
    shards, halves, share, columns = weight.shape
    rows = sum(piece[0].shape[0] for piece in pieces)
    in_specs = [
        pl.BlockSpec((shards, 1, share, columns), lambda j, p: (0, j, 0, 0)),
        pl.BlockSpec(inv_gain.shape, lambda j, p: (0, 0, 0)),
    ]
    args = [place, weight, inv_gain]
    for piece in pieces:
        for block in piece:
            in_specs.append(pl.BlockSpec(block.shape, lambda j, p: (0, 0)))
            args.append(block)
    return pl.pallas_call(
        functools.partial(project_kernel, shards * share, len(pieces)),
        out_shape=jax.ShapeDtypeStruct((rows, halves * columns), BF16),
        grid_spec=pltpu.PrefetchScalarGridSpec(
            num_scalar_prefetch=1,
            grid=(halves,),
            in_specs=in_specs,
            out_specs=pl.BlockSpec((rows, columns), lambda j, p: (0, j)),
            scratch_shapes=[pltpu.VMEM((rows, 1), F32)],
        ),
        compiler_params=pltpu.CompilerParams(vmem_limit_bytes=VMEM_LIMIT),
    )(*args)


def local(expert_out, kept_blocks, expert_ids, gate_levels, norm_gain, qkv_weight):
    parts = lax.axis_size("dp")
    experts = lax.axis_size("expert")
    tensors = lax.axis_size("tensor")
    part, mine, quarter_of = (lax.axis_index(a) for a in ("dp", "expert", "tensor"))
    devices = experts * tensors
    rows, quarter = expert_out.shape[1:]
    slots = rows // devices
    tok = expert_ids.shape[0]

    planes = parts // 2
    share, columns = qkv_weight.shape
    fetch = []
    for p in range(parts):
        for e in range(experts):
            source = (e + p // 2 + 4 * (p % 2)) % experts
            fetch.append((p * experts + source, p * experts + e))
    w = lax.dynamic_slice(qkv_weight, (0, lax.rem(part, 2) * (columns // 2)), (share, columns // 2))
    w = lax.ppermute(w, ("dp", "expert"), fetch)

    pieces = (3, 1)
    outgoing = list(pack(kept_blocks[0], expert_out[0].reshape(slots, devices, quarter), experts, pieces))

    ids = jnp.concatenate([expert_ids, gate_levels], axis=1)
    ids, w = lax.optimization_barrier((ids, w))
    ids = lax.all_gather(ids, "tensor")
    weight = lax.all_gather(w, "dp", axis=0, tiled=True).reshape(planes, 2, share, columns // 2)
    sel = select(ids, experts, slots)
    sel, outgoing[1] = lax.optimization_barrier((sel, outgoing[1]))

    gain = norm_gain.astype(F32)
    inv_gain = (1.0 / gain).reshape(tensors, 1, quarter)
    own_gain = lax.dynamic_slice(gain, (quarter_of * quarter,), (quarter,)).reshape(1, quarter)
    place = jnp.concatenate(
        [mine[None], (quarter_of - jnp.arange(tensors, dtype=jnp.int32)) % tensors]
    ).astype(jnp.int32)

    exchanged = []
    first = 0
    for packed in outgoing:
        n = packed.shape[1]
        arrived = lax.all_to_all(packed, "expert", 0, 0, tiled=True)
        own = combine(sel, first, arrived, own_gain)
        exchanged.append(
            [own]
            + [
                lax.ppermute(own, "tensor", [(i, (i + k) % tensors) for i in range(tensors)])
                for k in range(1, tensors)
            ]
        )
        first += n
    return project(place, exchanged, weight, inv_gain)


def solution(mesh):
    in_specs = (
        P("expert", "dp", "tensor"),
        P("expert", "dp"),
        P(("dp", "expert", "tensor"), None),
        P(("dp", "expert", "tensor"), None),
        P(),
        P("expert", "tensor"),
    )
    out_specs = P(("dp", "expert"), "tensor")
    return jax.shard_map(local, mesh=mesh, in_specs=in_specs, out_specs=out_specs, check_vma=False)
```

time: 176 us -> 142 us (0.81)
  the two profiles are of different devices: /device:TPU:10 before, /device:TPU:64 now
where the time goes in v2:
time: 142 us; the launch traced here: 141 us
  waiting for transfers between devices  55.6 us (39%)
  starting transfers between devices  33.4 us (24%)
  Pallas kernels  19.5 us (14%)
  between operations  13.6 us (10%)
  blocking collectives  11.1 us (8%)
  local copies, waits for them, and re-layouts  7.17 us (5%)
    all_to_all x2, waiting for transfers between devices, local(): arrived = lax.all_to_all(packed, 'expert', 0, 0, tiled=True)  37.2 us
    ppermute x6, starting transfers between devices, local(): lax.ppermute(own, 'tensor', [(i, (i + k) % tensors) for i in range(tensor...  19.4 us
    ppermute x6, waiting for transfers between devices, local(): lax.ppermute(own, 'tensor', [(i, (i + k) % tensors) for i in range(tensor...  18.3 us
    all_gather x1, blocking collectives, local(): ids = lax.all_gather(ids, 'tensor')  11.1 us
    pallas_call x1, Pallas kernels, project(): pl.pallas_call(functools.partial(project_kernel, shards * share, len(piec...  8.82 us
    all_to_all x2, starting transfers between devices, local(): arrived = lax.all_to_all(packed, 'expert', 0, 0, tiled=True)  8.53 us
    unnamed x22, local copies, waits for them, and re-layouts  6.17 us
    ppermute x1, starting transfers between devices, local(): w = lax.ppermute(w, ('dp', 'expert'), fetch)  5.38 us
  transfers between devices with their start and end apart: 10, of which 4 were waited for; matrix products, arithmetic and copies ran while one was open for 1% of the time, Pallas kernels for 8%

profile of v2, /device:TPU:64, one launch (start us, length us, event | category | flops | bytes accessed | tf_op | source)
XLA Modules:
  0.0 141.0 jit_solution(12588682133777873162)
XLA Ops:
  6.5 0.0 copy-start
  6.5 1.1 copy-done
  7.7 5.4 %collective-permute-start = (bf16[384,512]{1,0:T(8,128)(2,1)S(1)}, bf16[384,512]{1,0:T(8,128)(2,1)S(1)}, u32[]{:S(2)}, u32[]{:S(2)}) collective-permute-start(bf16[384,512]{1,0:T(8,128)(2,1)S(1)} %constant_dynamic-slice_fusion), channel_id=1, source_target_pairs={{0,0},{4,4},{8,8},{12,12},{16,16},{20,20},{24,24},{28,28},{48,32},... | collective-permute-start | bytes 1179656 | tf_op jit(solution)/shard_map/ppermute | solution.py:189
  13.1 5.3 %shard_map.65 = (bf16[8,3,48,768]{3,2,1,0:T(8,128)(2,1)}, bf16[8,1,48,768]{3,2,1,0:T(8,128)(2,1)}) custom-call(s32[12]{0:T(128)} %bitcast.10, bf16[48,32,768]{2,1,0:T(8,128)(2,1)} %bitcast.8), custom_call_target="tpu_custom_call" | custom-call | tf_op jit(solution)/shard_map/pallas_call | solution.py:42
  18.4 0.0 copy-start.9
  18.4 0.0 copy-start.10
  18.4 0.0 copy-start.8
  18.4 4.3 %all-to-all-start = ((bf16[8,3,48,768]{3,2,1,0:T(8,128)(2,1)}), bf16[8,3,48,768]{3,2,1,0:T(8,128)(2,1)S(1)}, u32[]{:S(2)}, u32[]{:S(2)}) async-start(bf16[8,3,48,768]{3,2,1,0:T(8,128)(2,1)} %get-tuple-element.15), calls=%async_computation | async-start | bytes 3538944 | tf_op jit(solution)/shard_map/all_to_all | solution.py:212
  22.8 0.0 all-gather.3.cloned.1.call-start
  22.8 0.0 copy-done.9
  22.8 0.0 copy-done.10
  22.9 0.0 collective-permute-done
  22.9 0.0 copy-start.7
  22.9 0.8 copy-done.7
  23.7 0.0 all-gather.3.cloned.1.call-update
  23.7 0.0 copy-done.8
  23.7 0.1 dynamic_slice.7
  23.8 11.1 %all-gather = s32[512,4]{0,1:T(4,128)S(1)} all-gather(s32[128,4]{0,1:T(4,128)S(1)} %pad_add_fusion), channel_id=2, replica_groups=mesh['dp'=16,'expert'=8,'tensor'=4] {'tensor'}, dimensions={0}, use_global_device_ids=true | all-gather | bytes 10240 | tf_op jit(solution)/shard_map/all_gather | solution.py:196
  34.9 0.9 copy.7
  35.8 3.5 %shard_map.64.sel_ref = bf16[4,128,384]{2,1,0:T(8,128)(2,1)} custom-call(s32[4,128,4]{2,1,0:T(8,128)} %bitcast.9), custom_call_target="tpu_custom_call" | custom-call | tf_op jit(solution)/shard_map/pallas_call | solution.py:78
  39.3 29.5 %all-to-all-done.rows_ref = bf16[8,3,48,768]{3,2,1,0:T(8,128)(2,1)S(1)} async-done(((bf16[8,3,48,768]{3,2,1,0:T(8,128)(2,1)}), bf16[8,3,48,768]{3,2,1,0:T(8,128)(2,1)S(1)}, u32[]{:S(2)}, u32[]{:S(2)}) %all-to-all-start) | async-done | bytes 1769504 | tf_op jit(solution)/shard_map/all_to_all | solution.py:212
  68.8 4.2 %all-to-all-start.1 = ((bf16[8,1,48,768]{3,2,1,0:T(8,128)(2,1)}), bf16[8,1,48,768]{3,2,1,0:T(8,128)(2,1)}, u32[]{:S(2)}, u32[]{:S(2)}) async-start(bf16[8,1,48,768]{3,2,1,0:T(8,128)(2,1)} %get-tuple-element.16), calls=%async_computation.1 | async-start | bytes 1179648 | tf_op jit(solution)/shard_map/all_to_all | solution.py:212
  73.0 0.0 copy-start.1
  73.0 1.0 copy-done.1
  74.0 0.0 copy-start.2
  74.0 0.5 shard_map.66.refs_0_
  74.5 4.7 %collective-permute-start.3 = (bf16[384,768]{1,0:T(8,128)(2,1)S(1)}, bf16[384,768]{1,0:T(8,128)(2,1)S(1)}, u32[]{:S(2)}, u32[]{:S(2)}) collective-permute-start(bf16[384,768]{1,0:T(8,128)(2,1)S(1)} %shard_map.66.refs_0_), channel_id=1, source_target_pairs={{0,3},{1,0},{2,1},{3,2},{4,7},{5,4},{6,5},{7,6},{8,11},{9,8},{10,9... | collective-permute-start | bytes 1769480 | tf_op jit(solution)/shard_map/ppermute | solution.py:217
  79.1 2.7 %collective-permute-start.2 = (bf16[384,768]{1,0:T(8,128)(2,1)S(1)}, bf16[384,768]{1,0:T(8,128)(2,1)S(1)}, u32[]{:S(2)}, u32[]{:S(2)}) collective-permute-start(bf16[384,768]{1,0:T(8,128)(2,1)S(1)} %shard_map.66.refs_0_), channel_id=1, source_target_pairs={{0,2},{1,3},{2,0},{3,1},{4,6},{5,7},{6,4},{7,5},{8,10},{9,11},{10,... | collective-permute-start | bytes 1769480 | tf_op jit(solution)/shard_map/ppermute | solution.py:217
  81.9 2.8 %collective-permute-start.1 = (bf16[384,768]{1,0:T(8,128)(2,1)S(1)}, bf16[384,768]{1,0:T(8,128)(2,1)S(1)}, u32[]{:S(2)}, u32[]{:S(2)}) collective-permute-start(bf16[384,768]{1,0:T(8,128)(2,1)S(1)} %shard_map.66.refs_0_), channel_id=1, source_target_pairs={{0,1},{1,2},{2,3},{3,0},{4,5},{5,6},{6,7},{7,4},{8,9},{9,10},{10,1... | collective-permute-start | bytes 1769480 | tf_op jit(solution)/shard_map/ppermute | solution.py:217
  84.7 7.7 %all-to-all-done.1.rows_ref = bf16[8,1,48,768]{3,2,1,0:T(8,128)(2,1)} async-done(((bf16[8,1,48,768]{3,2,1,0:T(8,128)(2,1)}), bf16[8,1,48,768]{3,2,1,0:T(8,128)(2,1)}, u32[]{:S(2)}, u32[]{:S(2)}) %all-to-all-start.1) | async-done | bytes 589856 | tf_op jit(solution)/shard_map/all_to_all | solution.py:212
  92.3 0.0 copy-done.2
  92.3 1.3 shard_map.67.refs_4_
  93.7 4.7 %collective-permute-start.6 = (bf16[128,768]{1,0:T(8,128)(2,1)S(1)}, bf16[128,768]{1,0:T(8,128)(2,1)S(1)}, u32[]{:S(2)}, u32[]{:S(2)}) collective-permute-start(bf16[128,768]{1,0:T(8,128)(2,1)S(1)} %shard_map.67.refs_4_), channel_id=1, source_target_pairs={{0,3},{1,0},{2,1},{3,2},{4,7},{5,4},{6,5},{7,6},{8,11},{9,8},{10,9... | collective-permute-start | bytes 589832 | tf_op jit(solution)/shard_map/ppermute | solution.py:217
  98.4 0.1 pad_add_fusion.1.place_ref
  98.4 2.7 %collective-permute-start.5 = (bf16[128,768]{1,0:T(8,128)(2,1)S(1)}, bf16[128,768]{1,0:T(8,128)(2,1)S(1)}, u32[]{:S(2)}, u32[]{:S(2)}) collective-permute-start(bf16[128,768]{1,0:T(8,128)(2,1)S(1)} %shard_map.67.refs_4_), channel_id=1, source_target_pairs={{0,2},{1,3},{2,0},{3,1},{4,6},{5,7},{6,4},{7,5},{8,10},{9,11},{10,... | collective-permute-start | bytes 589832 | tf_op jit(solution)/shard_map/ppermute | solution.py:217
  101.2 11.8 %collective-permute-done.6.refs_7_ = bf16[128,768]{1,0:T(8,128)(2,1)S(1)} collective-permute-done((bf16[128,768]{1,0:T(8,128)(2,1)S(1)}, bf16[128,768]{1,0:T(8,128)(2,1)S(1)}, u32[]{:S(2)}, u32[]{:S(2)}) %collective-permute-start.6) | collective-permute-done | bytes 196640 | tf_op jit(solution)/shard_map/ppermute | solution.py:217
  113.0 1.9 %collective-permute-start.4 = (bf16[128,768]{1,0:T(8,128)(2,1)S(1)}, bf16[128,768]{1,0:T(8,128)(2,1)S(1)}, u32[]{:S(2)}, u32[]{:S(2)}) collective-permute-start(bf16[128,768]{1,0:T(8,128)(2,1)S(1)} %shard_map.67.refs_4_), channel_id=1, source_target_pairs={{0,1},{1,2},{2,3},{3,0},{4,5},{5,6},{6,7},{7,4},{8,9},{9,10},{10,1... | collective-permute-start | bytes 589832 | tf_op jit(solution)/shard_map/ppermute | solution.py:217
  114.9 0.0 copy-start.3
  114.9 0.7 copy-done.3
  115.6 0.7 broadcast_divide_fusion
  116.3 0.0 collective-permute-done.5.refs_6_
  116.3 6.5 %collective-permute-done.4.refs_5_ = bf16[128,768]{1,0:T(8,128)(2,1)S(1)} collective-permute-done((bf16[128,768]{1,0:T(8,128)(2,1)S(1)}, bf16[128,768]{1,0:T(8,128)(2,1)S(1)}, u32[]{:S(2)}, u32[]{:S(2)}) %collective-permute-start.4) | collective-permute-done | bytes 196640 | tf_op jit(solution)/shard_map/ppermute | solution.py:217
  122.8 0.0 copy-start.5
  122.8 0.7 copy-done.5
  123.5 0.0 collective-permute-done.3.refs_3_
  123.5 0.0 collective-permute-done.2.refs_2_
  123.5 0.0 collective-permute-done.1.refs_1_
  123.5 0.0 all-gather.3.cloned.1.call-done
  123.5 0.0 copy-start.4
  123.5 0.9 copy-done.4
  124.4 0.0 copy-start.6
  124.4 0.9 copy-done.6
  125.4 8.8 %shard_map.68 = bf16[512,1024]{1,0:T(8,128)(2,1)} custom-call(s32[5]{0:T(128)S(1)} %pad_add_fusion.1.place_ref, bf16[8,2,384,512]{3,2,1,0:T(8,128)(2,1)} %bitcast.7, f32[4,1,768]{2,1,0:T(1,128)S(1)} %bitcast.6, bf16[384,768]{1,0:T(8,128)(2,1)S(1)} %shard_map.66.refs_0_, bf16[384,768]{1,0:T(8,128)(2,1)S(1)} %collective-permute-done.1.refs_1_, ...), custom_call_target="tpu_custom_call" | custom-call | tf_op jit(solution)/shard_map/pallas_call | solution.py:157
  (4 shorter events, 0.1 us)
Async XLA Ops:
  6.5 1.1 copy-start
  7.7 15.2 %collective-permute-start = (bf16[384,512]{1,0:T(8,128)(2,1)S(1)}, bf16[384,512]{1,0:T(8,128)(2,1)S(1)}, u32[]{:S(2)}, u32[]{:S(2)}) collective-permute-start(bf16[384,512]{1,0:T(8,128)(2,1)S(1)} %constant_dynamic-slice_fusion), channel_id=1, source_target_pairs={{0,0},{4,4},{8,8},{12,12},{16,16},{20,20},{24,24},{28,28},{48,32},... | collective-permute-start | bytes 1179656 | tf_op jit(solution)/shard_map/ppermute | solution.py:189
  18.4 4.4 %copy-start.9 = (s32[128,2]{0,1:T(2,128)S(1)}, s32[128,2]{0,1:T(2,128)}, u32[]{:S(2)}) copy-start(s32[128,2]{0,1:T(2,128)} %param.9) | copy-start | bytes 3076
  18.4 4.4 %copy-start.10 = (s32[128,2]{0,1:T(2,128)S(1)}, s32[128,2]{0,1:T(2,128)}, u32[]{:S(2)}) copy-start(s32[128,2]{0,1:T(2,128)} %param.8) | copy-start | bytes 3076
  18.4 5.3 %copy-start.8 = (bf16[3072]{0:T(1024)(128)(2,1)S(1)}, bf16[3072]{0:T(1024)(128)(2,1)}, u32[]{:S(2)}) copy-start(bf16[3072]{0:T(1024)(128)(2,1)} %param.10) | copy-start | bytes 18436
  18.4 50.3 %all-to-all-start = ((bf16[8,3,48,768]{3,2,1,0:T(8,128)(2,1)}), bf16[8,3,48,768]{3,2,1,0:T(8,128)(2,1)S(1)}, u32[]{:S(2)}, u32[]{:S(2)}) async-start(bf16[8,3,48,768]{3,2,1,0:T(8,128)(2,1)} %get-tuple-element.15), calls=%async_computation | async-start | bytes 3538944 | tf_op jit(solution)/shard_map/all_to_all | solution.py:212
  22.8 100.7 %all-gather.3.cloned.1.call-start = ((), (), s32[]{:S(2)}) async-start(), calls=%async_computation.2 | async-start | bytes 6684672 | tf_op jit(solution)/shard_map/all_gather | solution.py:197
  22.9 0.8 copy-start.7
  68.8 23.6 %all-to-all-start.1 = ((bf16[8,1,48,768]{3,2,1,0:T(8,128)(2,1)}), bf16[8,1,48,768]{3,2,1,0:T(8,128)(2,1)}, u32[]{:S(2)}, u32[]{:S(2)}) async-start(bf16[8,1,48,768]{3,2,1,0:T(8,128)(2,1)} %get-tuple-element.16), calls=%async_computation.1 | async-start | bytes 1179648 | tf_op jit(solution)/shard_map/all_to_all | solution.py:212
  73.0 1.0 copy-start.1
  74.0 18.3 %copy-start.2 = (bf16[4,128,384]{2,1,0:T(8,128)(2,1)S(1)}, bf16[4,128,384]{2,1,0:T(8,128)(2,1)}, u32[]{:S(2)}) copy-start(bf16[4,128,384]{2,1,0:T(8,128)(2,1)} %shard_map.64.sel_ref) | copy-start | bytes 1179652
  74.5 49.0 %collective-permute-start.3 = (bf16[384,768]{1,0:T(8,128)(2,1)S(1)}, bf16[384,768]{1,0:T(8,128)(2,1)S(1)}, u32[]{:S(2)}, u32[]{:S(2)}) collective-permute-start(bf16[384,768]{1,0:T(8,128)(2,1)S(1)} %shard_map.66.refs_0_), channel_id=1, source_target_pairs={{0,3},{1,0},{2,1},{3,2},{4,7},{5,4},{6,5},{7,6},{8,11},{9,8},{10,9... | collective-permute-start | bytes 1769480 | tf_op jit(solution)/shard_map/ppermute | solution.py:217
  79.1 44.3 %collective-permute-start.2 = (bf16[384,768]{1,0:T(8,128)(2,1)S(1)}, bf16[384,768]{1,0:T(8,128)(2,1)S(1)}, u32[]{:S(2)}, u32[]{:S(2)}) collective-permute-start(bf16[384,768]{1,0:T(8,128)(2,1)S(1)} %shard_map.66.refs_0_), channel_id=1, source_target_pairs={{0,2},{1,3},{2,0},{3,1},{4,6},{5,7},{6,4},{7,5},{8,10},{9,11},{10,... | collective-permute-start | bytes 1769480 | tf_op jit(solution)/shard_map/ppermute | solution.py:217
  81.9 41.6 %collective-permute-start.1 = (bf16[384,768]{1,0:T(8,128)(2,1)S(1)}, bf16[384,768]{1,0:T(8,128)(2,1)S(1)}, u32[]{:S(2)}, u32[]{:S(2)}) collective-permute-start(bf16[384,768]{1,0:T(8,128)(2,1)S(1)} %shard_map.66.refs_0_), channel_id=1, source_target_pairs={{0,1},{1,2},{2,3},{3,0},{4,5},{5,6},{6,7},{7,4},{8,9},{9,10},{10,1... | collective-permute-start | bytes 1769480 | tf_op jit(solution)/shard_map/ppermute | solution.py:217
  93.7 19.3 %collective-permute-start.6 = (bf16[128,768]{1,0:T(8,128)(2,1)S(1)}, bf16[128,768]{1,0:T(8,128)(2,1)S(1)}, u32[]{:S(2)}, u32[]{:S(2)}) collective-permute-start(bf16[128,768]{1,0:T(8,128)(2,1)S(1)} %shard_map.67.refs_4_), channel_id=1, source_target_pairs={{0,3},{1,0},{2,1},{3,2},{4,7},{5,4},{6,5},{7,6},{8,11},{9,8},{10,9... | collective-permute-start | bytes 589832 | tf_op jit(solution)/shard_map/ppermute | solution.py:217
  98.4 17.8 %collective-permute-start.5 = (bf16[128,768]{1,0:T(8,128)(2,1)S(1)}, bf16[128,768]{1,0:T(8,128)(2,1)S(1)}, u32[]{:S(2)}, u32[]{:S(2)}) collective-permute-start(bf16[128,768]{1,0:T(8,128)(2,1)S(1)} %shard_map.67.refs_4_), channel_id=1, source_target_pairs={{0,2},{1,3},{2,0},{3,1},{4,6},{5,7},{6,4},{7,5},{8,10},{9,11},{10,... | collective-permute-start | bytes 589832 | tf_op jit(solution)/shard_map/ppermute | solution.py:217
  113.0 9.8 %collective-permute-start.4 = (bf16[128,768]{1,0:T(8,128)(2,1)S(1)}, bf16[128,768]{1,0:T(8,128)(2,1)S(1)}, u32[]{:S(2)}, u32[]{:S(2)}) collective-permute-start(bf16[128,768]{1,0:T(8,128)(2,1)S(1)} %shard_map.67.refs_4_), channel_id=1, source_target_pairs={{0,1},{1,2},{2,3},{3,0},{4,5},{5,6},{6,7},{7,4},{8,9},{9,10},{10,1... | collective-permute-start | bytes 589832 | tf_op jit(solution)/shard_map/ppermute | solution.py:217
  114.9 0.7 copy-start.3
  122.8 0.7 copy-start.5
  123.5 0.9 copy-start.4
  124.4 0.9 copy-start.6
Sparse Core Ops, SparseCore 0:
  25.7 62.0 all-gather.2

commit v3 on v1

--- a/solution.py
+++ b/solution.py
@@ -9,7 +9,43 @@
 
 F32 = jnp.float32
 BF16 = jnp.bfloat16
-VMEM_LIMIT = 48 * 1024 * 1024
+VMEM_LIMIT = 60 * 1024 * 1024
+
+
+def pack_kernel(tensors, first, kept_ref, rows_ref, out_ref):
+    slots, owners, width = rows_ref.shape
+    experts, count = out_ref.shape[:2]
+    per_block = 4
+    blocks = slots // per_block
+    step = pl.program_id(0)
+    row = lax.broadcasted_iota(jnp.int32, (experts * count * slots, 1), 0)
+    slot, group = lax.rem(row, slots), lax.div(row, slots)
+    owner = lax.div(group, count) * tensors + first + lax.rem(group, count)
+    col = lax.broadcasted_iota(jnp.int32, (experts * count * slots, slots * owners), 1)
+    move = (col == slot * owners + owner).astype(F32).astype(BF16)
+    rows = [
+        rows_ref[b * per_block : (b + 1) * per_block].reshape(per_block * owners, width)
+        * (kept_ref[step * blocks + b] != 0).astype(F32).astype(BF16)
+        for b in range(blocks)
+    ]
+    moved = jnp.dot(move, jnp.concatenate(rows, axis=0), preferred_element_type=F32)
+    out_ref[...] = moved.astype(BF16).reshape(experts, count, slots, width)
+
+
+def pack(kept, rows, experts, first, count):
+    slots, owners, width = rows.shape
+    step = 16
+    return pl.pallas_call(
+        functools.partial(pack_kernel, owners // experts, first),
+        out_shape=jax.ShapeDtypeStruct((experts, count, slots, width), BF16),
+        grid_spec=pltpu.PrefetchScalarGridSpec(
+            num_scalar_prefetch=1,
+            grid=(slots // step,),
+            in_specs=[pl.BlockSpec((step, owners, width), lambda j, k: (j, 0, 0))],
+            out_specs=pl.BlockSpec((experts, count, step, width), lambda j, k: (0, 0, j, 0)),
+        ),
+        compiler_params=pltpu.CompilerParams(vmem_limit_bytes=VMEM_LIMIT),
+    )(kept, rows)
 
 
 def select_kernel(experts, slots, ids_ref, sel_ref):
@@ -50,40 +86,55 @@
         out_ref[pl.ds(q * tok, tok), :] = (total * gain_ref[...]).astype(BF16)
 
 
-def combine(sel, rows, gain):
-    owners, tok, _ = sel.shape
+def combine(sel, first, rows, gain):
+    tok, cols = sel.shape[1:]
+    experts, owners, slots, width = rows.shape
     return pl.pallas_call(
         combine_kernel,
-        out_shape=jax.ShapeDtypeStruct((owners * tok, rows.shape[3]), BF16),
+        out_shape=jax.ShapeDtypeStruct((owners * tok, width), BF16),
+        grid=(1,),
+        in_specs=[
+            pl.BlockSpec((owners, tok, cols), lambda i: (first // owners, 0, 0)),
+            pl.BlockSpec(rows.shape, lambda i: (0, 0, 0, 0)),
+            pl.BlockSpec(gain.shape, lambda i: (0, 0)),
+        ],
+        out_specs=pl.BlockSpec((owners * tok, width), lambda i: (0, 0)),
+        cost_estimate=pl.CostEstimate(flops=50_625_000_000, bytes_accessed=0, transcendentals=0),
+        compiler_params=pltpu.CompilerParams(vmem_limit_bytes=VMEM_LIMIT),
     )(sel, rows, gain)
 
 
 def project_kernel(width, place_ref, own_ref, one_ref, two_ref, three_ref, w_ref, inv_ref, *rest):
     out_ref, scale_ref = rest[-2:]
     blocks = (own_ref, one_ref, two_ref, three_ref)
-
-    @pl.when(pl.program_id(0) == 0)
+    half = pl.program_id(0)
+
+    @pl.when(half == 0)
     def _():
         total = jnp.zeros(scale_ref.shape, F32)
         for k, block in enumerate(blocks):
-            plain = block[...].astype(F32) * inv_ref[place_ref[k]]
+            plain = block[...].astype(F32) * inv_ref[place_ref[1 + k]]
             total = total + jnp.sum(plain * plain, axis=1, keepdims=True)
         scale_ref[...] = lax.rsqrt(total / width + 1e-05)
 
-    acc = jnp.dot(own_ref[...], w_ref[place_ref[0]], preferred_element_type=F32)
-    for k in range(1, 4):
-        acc = acc + jnp.dot(blocks[k][...], w_ref[place_ref[k]], preferred_element_type=F32)
+    shards, _, share, _ = w_ref.shape
+    acc = None
+    for k, block in enumerate(blocks):
+        for i in range(2):
+            shard = 2 * place_ref[1 + k] + i
+            at = lax.rem(shard - place_ref[0] + 4 * half + shards, shards)
+            term = jnp.dot(block[:, i * share : (i + 1) * share], w_ref[at, 0], preferred_element_type=F32)
+            acc = term if acc is None else acc + term
     out_ref[...] = (acc * scale_ref[...]).astype(BF16)
 
 
 def project(place, blocks, weight, inv_gain, total_rows, row_block, into=None):
     rows, quarter = blocks[0].shape
-    parts, _, columns = weight.shape
-    tile = 256
+    shards, halves, share, columns = weight.shape
     whole = pl.BlockSpec((rows, quarter), lambda j, p: (0, 0))
     in_specs = [whole] * 4 + [
-        pl.BlockSpec((parts, quarter, tile), lambda j, p: (0, 0, j)),
-        pl.BlockSpec((parts, 1, quarter), lambda j, p: (0, 0, 0)),
+        pl.BlockSpec((shards, 1, share, columns), lambda j, p: (0, j, 0, 0)),
+        pl.BlockSpec(inv_gain.shape, lambda j, p: (0, 0, 0)),
     ]
     args = [place, *blocks, weight, inv_gain]
     aliases = {}
@@ -92,13 +143,13 @@
         aliases = {len(args): 0}
         args.append(into)
     return pl.pallas_call(
-        functools.partial(project_kernel, parts * quarter),
-        out_shape=jax.ShapeDtypeStruct((total_rows, columns), BF16),
+        functools.partial(project_kernel, 4 * quarter),
+        out_shape=jax.ShapeDtypeStruct((total_rows, halves * columns), BF16),
         grid_spec=pltpu.PrefetchScalarGridSpec(
             num_scalar_prefetch=1,
-            grid=(columns // tile,),
+            grid=(halves,),
             in_specs=in_specs,
-            out_specs=pl.BlockSpec((rows, tile), lambda j, p: (row_block, j)),
+            out_specs=pl.BlockSpec((rows, columns), lambda j, p: (row_block, j)),
             scratch_shapes=[pltpu.VMEM((rows, 1), F32)],
         ),
         input_output_aliases=aliases,
@@ -116,42 +167,46 @@
     slots = rows // devices
     tok = expert_ids.shape[0]
 
-    share = qkv_weight.shape[0] // parts
-    columns = qkv_weight.shape[1]
-    w = lax.dynamic_slice(qkv_weight, (part * share, 0), (share, columns))
-    w = w.reshape(1, 1, 1, share, columns)
-    for axis, step in enumerate((4, 2, 1)):
-        other = lax.ppermute(w, "expert", [(i, i ^ step) for i in range(experts)])
-        upper = (mine & step) != 0
-        w = jnp.concatenate([jnp.where(upper, other, w), jnp.where(upper, w, other)], axis=axis)
-    w = lax.all_gather(w.reshape(experts * share, columns), "dp", axis=0, tiled=True)
-    weight = (
-        w.reshape(parts, experts, share, columns)
-        .transpose(1, 0, 2, 3)
-        .reshape(tensors, quarter, columns)
-    )
-
-    mask = jnp.repeat(kept_blocks[0], 4 * devices).astype(BF16)
-    masked = (expert_out[0] * mask[:, None]).reshape(slots, experts, tensors, quarter)
-    outgoing = masked.transpose(1, 2, 0, 3)
-
-    ids = lax.all_gather(jnp.concatenate([expert_ids, gate_levels], axis=1), "tensor")
+    planes = parts // 2
+    share, columns = qkv_weight.shape
+    fetch = []
+    for p in range(parts):
+        for e in range(experts):
+            source = (e + p // 2 + 4 * (p % 2)) % experts
+            fetch.append((p * experts + source, p * experts + e))
+    w = lax.dynamic_slice(qkv_weight, (0, lax.rem(part, 2) * (columns // 2)), (share, columns // 2))
+    w = lax.ppermute(w, ("dp", "expert"), fetch)
+
+    pieces = (2, 2)
+    slotted = expert_out[0].reshape(slots, devices, quarter)
+    outgoing = [pack(kept_blocks[0], slotted, experts, sum(pieces[:i]), n) for i, n in enumerate(pieces)]
+
+    ids = jnp.concatenate([expert_ids, gate_levels], axis=1)
+    ids, w = lax.optimization_barrier((ids, w))
+    ids = lax.all_gather(ids, "tensor")
+    weight = lax.all_gather(w, "dp", axis=0, tiled=True).reshape(planes, 2, share, columns // 2)
     sel = select(ids, experts, slots)
+    sel, outgoing[1] = lax.optimization_barrier((sel, outgoing[1]))
 
     gain = norm_gain.astype(F32)
     inv_gain = (1.0 / gain).reshape(tensors, 1, quarter)
     own_gain = lax.dynamic_slice(gain, (quarter_of * quarter,), (quarter,)).reshape(1, quarter)
-    place = (quarter_of - jnp.arange(tensors, dtype=jnp.int32)) % tensors
+    place = jnp.concatenate(
+        [mine[None], (quarter_of - jnp.arange(tensors, dtype=jnp.int32)) % tensors]
+    ).astype(jnp.int32)
 
     out = None
-    for lo, hi in ((0, 3), (3, 4)):
-        arrived = lax.all_to_all(outgoing[:, lo:hi], "expert", 0, 0, tiled=True)
-        own = combine(sel[lo:hi], arrived, own_gain)
+    first = 0
+    for packed in outgoing:
+        n = packed.shape[1]
+        arrived = lax.all_to_all(packed, "expert", 0, 0, tiled=True)
+        own = combine(sel, first, arrived, own_gain)
         blocks = [own] + [
             lax.ppermute(own, "tensor", [(i, (i + k) % tensors) for i in range(tensors)])
             for k in range(1, tensors)
         ]
-        out = project(place, blocks, weight, inv_gain, tensors * tok, lo // (hi - lo), out)
+        out = project(place, blocks, weight, inv_gain, tensors * tok, first // n, out)
+        first += n
     return out
 
 

time: 176 us -> 137 us (0.78)
  the two profiles are of different devices: /device:TPU:10 before, /device:TPU:321 now
where the time goes in v3:
time: 137 us
  waiting for transfers between devices  41.6 us (30%)
  starting transfers between devices  33.8 us (25%)
  Pallas kernels  31.2 us (23%)
  between operations  13.6 us (10%)
  blocking collectives  9.14 us (7%)
  local copies, waits for them, and re-layouts  6.13 us (4%)
    all_to_all x2, waiting for transfers between devices, local(): arrived = lax.all_to_all(packed, 'expert', 0, 0, tiled=True)  32.4 us
    ppermute x6, starting transfers between devices, local(): lax.ppermute(own, 'tensor', [(i, (i + k) % tensors) for i in range(tensor...  21 us
    pallas_call x2, Pallas kernels, project(): pl.pallas_call(functools.partial(project_kernel, 4 * quarter), out_shape=...  13.4 us
    pallas_call x2, Pallas kernels, pack(): pl.pallas_call(functools.partial(pack_kernel, owners // experts, first),...  9.52 us
    ppermute x6, waiting for transfers between devices, local(): lax.ppermute(own, 'tensor', [(i, (i + k) % tensors) for i in range(tensor...  9.18 us
    all_gather x1, blocking collectives, local(): ids = lax.all_gather(ids, 'tensor')  9.14 us
    all_to_all x2, starting transfers between devices, local(): arrived = lax.all_to_all(packed, 'expert', 0, 0, tiled=True)  7.61 us
    ppermute x1, starting transfers between devices, local(): w = lax.ppermute(w, ('dp', 'expert'), fetch)  5.1 us
  transfers between devices with their start and end apart: 10, of which 4 were waited for; matrix products, arithmetic and copies ran while one was open for 2% of the time, Pallas kernels for 18%

profile of v3, /device:TPU:321, one launch (start us, length us, event | category | flops | bytes accessed | tf_op | source)
XLA Modules:
  0.0 136.8 jit_solution(3461664804667708758)
XLA Ops:
  6.5 0.0 copy-start
  6.5 1.1 copy-done
  7.7 5.1 %collective-permute-start = (bf16[384,512]{1,0:T(8,128)(2,1)S(1)}, bf16[384,512]{1,0:T(8,128)(2,1)S(1)}, u32[]{:S(2)}, u32[]{:S(2)}) collective-permute-start(bf16[384,512]{1,0:T(8,128)(2,1)S(1)} %constant_dynamic-slice_fusion), channel_id=1, source_target_pairs={{0,0},{4,4},{8,8},{12,12},{16,16},{20,20},{24,24},{28,28},{48,32},... | collective-permute-start | bytes 1179656 | tf_op jit(solution)/shard_map/ppermute | solution.py:178
  12.8 4.7 %shard_map.67 = bf16[8,2,48,768]{3,2,1,0:T(8,128)(2,1)} custom-call(s32[12]{0:T(128)} %bitcast.13, bf16[48,32,768]{2,1,0:T(8,128)(2,1)} %bitcast.8), custom_call_target="tpu_custom_call" | custom-call | tf_op jit(solution)/shard_map/pallas_call | solution.py:38
  17.5 0.0 copy-start.11
  17.5 0.0 copy-start.12
  17.5 4.0 %all-to-all-start.1 = ((bf16[8,2,48,768]{3,2,1,0:T(8,128)(2,1)}), bf16[8,2,48,768]{3,2,1,0:T(8,128)(2,1)S(1)}, u32[]{:S(2)}, u32[]{:S(2)}) async-start(bf16[8,2,48,768]{3,2,1,0:T(8,128)(2,1)} %shard_map.67), calls=%async_computation.1 | async-start | bytes 2359296 | tf_op jit(solution)/shard_map/all_to_all | solution.py:202
  21.6 0.0 all-gather.3.cloned.1.call-start
  21.6 0.0 copy-done.11
  21.6 0.0 copy-done.12
  21.6 0.0 collective-permute-done
  21.7 0.0 copy-start.9
  21.7 0.8 copy-done.9
  22.5 0.0 all-gather.3.cloned.1.call-update
  22.5 0.0 copy-start.10
  22.5 4.8 %shard_map.65 = bf16[8,2,48,768]{3,2,1,0:T(8,128)(2,1)} custom-call(s32[12]{0:T(128)} %bitcast.14, bf16[48,32,768]{2,1,0:T(8,128)(2,1)} %bitcast.9), custom_call_target="tpu_custom_call" | custom-call | tf_op jit(solution)/shard_map/pallas_call | solution.py:38
  27.3 0.0 copy-done.10
  27.3 0.1 dynamic_slice.7
  27.4 0.6 reshape.9.gain_ref
  28.0 9.1 %all-gather = s32[512,4]{0,1:T(4,128)S(1)} all-gather(s32[128,4]{0,1:T(4,128)S(1)} %pad_add_fusion), channel_id=2, replica_groups=mesh['dp'=16,'expert'=8,'tensor'=4] {'tensor'}, dimensions={0}, use_global_device_ids=true | all-gather | bytes 10240 | tf_op jit(solution)/shard_map/all_gather | solution.py:186
  37.1 0.9 copy.8
  38.0 3.5 %shard_map.64.sel_ref = bf16[4,128,384]{2,1,0:T(8,128)(2,1)} custom-call(s32[4,128,4]{2,1,0:T(8,128)} %bitcast.10), custom_call_target="tpu_custom_call" | custom-call | tf_op jit(solution)/shard_map/pallas_call | solution.py:74
  41.4 14.7 %all-to-all-done.1.rows_ref = bf16[8,2,48,768]{3,2,1,0:T(8,128)(2,1)S(1)} async-done(((bf16[8,2,48,768]{3,2,1,0:T(8,128)(2,1)}), bf16[8,2,48,768]{3,2,1,0:T(8,128)(2,1)S(1)}, u32[]{:S(2)}, u32[]{:S(2)}) %all-to-all-start.1) | async-done | bytes 1179680 | tf_op jit(solution)/shard_map/all_to_all | solution.py:202
  56.1 0.0 copy-start.1
  56.1 3.6 %all-to-all-start = ((bf16[8,2,48,768]{3,2,1,0:T(8,128)(2,1)}), bf16[8,2,48,768]{3,2,1,0:T(8,128)(2,1)S(1)}, u32[]{:S(2)}, u32[]{:S(2)}) async-start(bf16[8,2,48,768]{3,2,1,0:T(8,128)(2,1)} %shard_map.65), calls=%async_computation | async-start | bytes 2359296 | tf_op jit(solution)/shard_map/all_to_all | solution.py:202
  59.7 0.0 copy-done.1
  59.7 2.4 %shard_map.68.own_ref = bf16[256,768]{1,0:T(8,128)(2,1)} custom-call(bf16[4,128,384]{2,1,0:T(8,128)(2,1)} %shard_map.64.sel_ref, bf16[8,2,48,768]{3,2,1,0:T(8,128)(2,1)} %copy-done.1, f32[1,768]{1,0:T(1,128)} %reshape.9.gain_ref), custom_call_target="tpu_custom_call" | custom-call | flops 50624999424 | tf_op jit(solution)/shard_map/pallas_call | solution.py:92
  62.2 4.4 %collective-permute-start.6 = (bf16[256,768]{1,0:T(8,128)(2,1)}, bf16[256,768]{1,0:T(8,128)(2,1)S(1)}, u32[]{:S(2)}, u32[]{:S(2)}) collective-permute-start(bf16[256,768]{1,0:T(8,128)(2,1)} %shard_map.68.own_ref), channel_id=1, source_target_pairs={{0,3},{1,0},{2,1},{3,2},{4,7},{5,4},{6,5},{7,6},{8,11},{9,8},{10,9... | collective-permute-start | bytes 1179656 | tf_op jit(solution)/shard_map/ppermute | solution.py:205
  66.5 2.4 %collective-permute-start.5 = (bf16[256,768]{1,0:T(8,128)(2,1)}, bf16[256,768]{1,0:T(8,128)(2,1)S(1)}, u32[]{:S(2)}, u32[]{:S(2)}) collective-permute-start(bf16[256,768]{1,0:T(8,128)(2,1)} %shard_map.68.own_ref), channel_id=1, source_target_pairs={{0,2},{1,3},{2,0},{3,1},{4,6},{5,7},{6,4},{7,5},{8,10},{9,11},{10,... | collective-permute-start | bytes 1179656 | tf_op jit(solution)/shard_map/ppermute | solution.py:205
  69.0 2.5 %collective-permute-start.4 = (bf16[256,768]{1,0:T(8,128)(2,1)}, bf16[256,768]{1,0:T(8,128)(2,1)S(1)}, u32[]{:S(2)}, u32[]{:S(2)}) collective-permute-start(bf16[256,768]{1,0:T(8,128)(2,1)} %shard_map.68.own_ref), channel_id=1, source_target_pairs={{0,1},{1,2},{2,3},{3,0},{4,5},{5,6},{6,7},{7,4},{8,9},{9,10},{10,1... | collective-permute-start | bytes 1179656 | tf_op jit(solution)/shard_map/ppermute | solution.py:205
  71.5 17.7 %all-to-all-done.rows_ref = bf16[8,2,48,768]{3,2,1,0:T(8,128)(2,1)S(1)} async-done(((bf16[8,2,48,768]{3,2,1,0:T(8,128)(2,1)}), bf16[8,2,48,768]{3,2,1,0:T(8,128)(2,1)S(1)}, u32[]{:S(2)}, u32[]{:S(2)}) %all-to-all-start) | async-done | bytes 1179680 | tf_op jit(solution)/shard_map/all_to_all | solution.py:202
  89.2 0.0 copy-start.2
  89.2 1.0 copy-done.2
  90.2 2.4 %shard_map.66.own_ref = bf16[256,768]{1,0:T(8,128)(2,1)} custom-call(bf16[4,128,384]{2,1,0:T(8,128)(2,1)} %shard_map.64.sel_ref, bf16[8,2,48,768]{3,2,1,0:T(8,128)(2,1)} %copy-done.2, f32[1,768]{1,0:T(1,128)} %reshape.9.gain_ref), custom_call_target="tpu_custom_call" | custom-call | flops 50624999424 | tf_op jit(solution)/shard_map/pallas_call | solution.py:92
  92.6 6.8 %collective-permute-start.3 = (bf16[256,768]{1,0:T(8,128)(2,1)}, bf16[256,768]{1,0:T(8,128)(2,1)S(1)}, u32[]{:S(2)}, u32[]{:S(2)}) collective-permute-start(bf16[256,768]{1,0:T(8,128)(2,1)} %shard_map.66.own_ref), channel_id=1, source_target_pairs={{0,3},{1,0},{2,1},{3,2},{4,7},{5,4},{6,5},{7,6},{8,11},{9,8},{10,9... | collective-permute-start | bytes 1179656 | tf_op jit(solution)/shard_map/ppermute | solution.py:205
  99.4 2.2 %collective-permute-start.2 = (bf16[256,768]{1,0:T(8,128)(2,1)}, bf16[256,768]{1,0:T(8,128)(2,1)S(1)}, u32[]{:S(2)}, u32[]{:S(2)}) collective-permute-start(bf16[256,768]{1,0:T(8,128)(2,1)} %shard_map.66.own_ref), channel_id=1, source_target_pairs={{0,2},{1,3},{2,0},{3,1},{4,6},{5,7},{6,4},{7,5},{8,10},{9,11},{10,... | collective-permute-start | bytes 1179656 | tf_op jit(solution)/shard_map/ppermute | solution.py:205
  101.6 0.0 collective-permute-done.6.three_ref
  101.6 0.0 copy-start.3
  101.6 2.8 %collective-permute-start.1 = (bf16[256,768]{1,0:T(8,128)(2,1)}, bf16[256,768]{1,0:T(8,128)(2,1)S(1)}, u32[]{:S(2)}, u32[]{:S(2)}) collective-permute-start(bf16[256,768]{1,0:T(8,128)(2,1)} %shard_map.66.own_ref), channel_id=1, source_target_pairs={{0,1},{1,2},{2,3},{3,0},{4,5},{5,6},{6,7},{7,4},{8,9},{9,10},{10,1... | collective-permute-start | bytes 1179656 | tf_op jit(solution)/shard_map/ppermute | solution.py:205
  104.4 0.7 pad_add_fusion.1.place_ref
  105.1 0.6 broadcast_divide_fusion
  105.7 0.0 collective-permute-done.5.two_ref
  105.7 0.0 copy-start.4
  105.7 0.0 collective-permute-done.4.one_ref
  105.7 0.0 copy-start.5
  105.7 0.0 all-gather.3.cloned.1.call-done
  105.7 0.0 copy-done.3
  105.7 0.7 copy-done.4
  106.4 0.2 copy-done.5
  106.6 6.7 %shard_map.69.rest_0_ = bf16[512,1024]{1,0:T(8,128)(2,1)} custom-call(s32[5]{0:T(128)} %pad_add_fusion.1.place_ref, bf16[256,768]{1,0:T(8,128)(2,1)} %shard_map.68.own_ref, bf16[256,768]{1,0:T(8,128)(2,1)} %copy-done.5, bf16[256,768]{1,0:T(8,128)(2,1)} %copy-done.4, bf16[256,768]{1,0:T(8,128)(2,1)} %copy-done.3, bf16[8,2,384,512]{3,2,1,0:T(8,128)(2,1)} %bitcast.6, ...), custom_call_target="tpu_custom_call" | custom-call | tf_op jit(solution)/shard_map/pallas_call | solution.py:145
  113.3 2.8 %collective-permute-done.3.three_ref = bf16[256,768]{1,0:T(8,128)(2,1)S(1)} collective-permute-done((bf16[256,768]{1,0:T(8,128)(2,1)}, bf16[256,768]{1,0:T(8,128)(2,1)S(1)}, u32[]{:S(2)}, u32[]{:S(2)}) %collective-permute-start.3) | collective-permute-done | bytes 393248 | tf_op jit(solution)/shard_map/ppermute | solution.py:205
  116.1 0.0 copy-start.6
  116.1 0.0 collective-permute-done.2.two_ref
  116.1 0.0 copy-start.7
  116.1 6.4 %collective-permute-done.1.one_ref = bf16[256,768]{1,0:T(8,128)(2,1)S(1)} collective-permute-done((bf16[256,768]{1,0:T(8,128)(2,1)}, bf16[256,768]{1,0:T(8,128)(2,1)S(1)}, u32[]{:S(2)}, u32[]{:S(2)}) %collective-permute-start.1) | collective-permute-done | bytes 393248 | tf_op jit(solution)/shard_map/ppermute | solution.py:205
  122.5 0.0 copy-done.6
  122.5 0.0 copy-done.7
  122.5 0.0 copy-start.8
  122.5 0.8 copy-done.8
  123.2 6.7 %shard_map.70 = bf16[512,1024]{1,0:T(8,128)(2,1)} custom-call(s32[5]{0:T(128)} %pad_add_fusion.1.place_ref, bf16[256,768]{1,0:T(8,128)(2,1)} %shard_map.66.own_ref, bf16[256,768]{1,0:T(8,128)(2,1)} %copy-done.8, bf16[256,768]{1,0:T(8,128)(2,1)} %copy-done.7, bf16[256,768]{1,0:T(8,128)(2,1)} %copy-done.6, ...), custom_call_target="tpu_custom_call", output_to_operand_aliasing={{}: (7, {})} | custom-call | tf_op jit(solution)/shard_map/pallas_call | solution.py:145
  (3 shorter events, 0.0 us)
Async XLA Ops:
  6.5 1.1 copy-start
  7.7 14.0 %collective-permute-start = (bf16[384,512]{1,0:T(8,128)(2,1)S(1)}, bf16[384,512]{1,0:T(8,128)(2,1)S(1)}, u32[]{:S(2)}, u32[]{:S(2)}) collective-permute-start(bf16[384,512]{1,0:T(8,128)(2,1)S(1)} %constant_dynamic-slice_fusion), channel_id=1, source_target_pairs={{0,0},{4,4},{8,8},{12,12},{16,16},{20,20},{24,24},{28,28},{48,32},... | collective-permute-start | bytes 1179656 | tf_op jit(solution)/shard_map/ppermute | solution.py:178
  17.5 4.1 %copy-start.11 = (s32[128,2]{0,1:T(2,128)S(1)}, s32[128,2]{0,1:T(2,128)}, u32[]{:S(2)}) copy-start(s32[128,2]{0,1:T(2,128)} %param.9) | copy-start | bytes 3076
  17.5 4.1 %copy-start.12 = (s32[128,2]{0,1:T(2,128)S(1)}, s32[128,2]{0,1:T(2,128)}, u32[]{:S(2)}) copy-start(s32[128,2]{0,1:T(2,128)} %param.8) | copy-start | bytes 3076
  17.5 38.6 %all-to-all-start.1 = ((bf16[8,2,48,768]{3,2,1,0:T(8,128)(2,1)}), bf16[8,2,48,768]{3,2,1,0:T(8,128)(2,1)S(1)}, u32[]{:S(2)}, u32[]{:S(2)}) async-start(bf16[8,2,48,768]{3,2,1,0:T(8,128)(2,1)} %shard_map.67), calls=%async_computation.1 | async-start | bytes 2359296 | tf_op jit(solution)/shard_map/all_to_all | solution.py:202
  21.6 84.1 %all-gather.3.cloned.1.call-start = ((), (), s32[]{:S(2)}) async-start(), calls=%async_computation.2 | async-start | bytes 6684672 | tf_op jit(solution)/shard_map/all_gather | solution.py:187
  21.7 0.8 copy-start.9
  22.5 4.8 %copy-start.10 = (bf16[3072]{0:T(1024)(128)(2,1)S(1)}, bf16[3072]{0:T(1024)(128)(2,1)}, u32[]{:S(2)}) copy-start(bf16[3072]{0:T(1024)(128)(2,1)} %param.10) | copy-start | bytes 18436
  56.1 3.6 %copy-start.1 = (bf16[8,2,48,768]{3,2,1,0:T(8,128)(2,1)}, bf16[8,2,48,768]{3,2,1,0:T(8,128)(2,1)S(1)}, u32[]{:S(2)}) copy-start(bf16[8,2,48,768]{3,2,1,0:T(8,128)(2,1)S(1)} %all-to-all-done.1.rows_ref) | copy-start | bytes 3538948
  56.1 33.1 %all-to-all-start = ((bf16[8,2,48,768]{3,2,1,0:T(8,128)(2,1)}), bf16[8,2,48,768]{3,2,1,0:T(8,128)(2,1)S(1)}, u32[]{:S(2)}, u32[]{:S(2)}) async-start(bf16[8,2,48,768]{3,2,1,0:T(8,128)(2,1)} %shard_map.65), calls=%async_computation | async-start | bytes 2359296 | tf_op jit(solution)/shard_map/all_to_all | solution.py:202
  62.2 39.4 %collective-permute-start.6 = (bf16[256,768]{1,0:T(8,128)(2,1)}, bf16[256,768]{1,0:T(8,128)(2,1)S(1)}, u32[]{:S(2)}, u32[]{:S(2)}) collective-permute-start(bf16[256,768]{1,0:T(8,128)(2,1)} %shard_map.68.own_ref), channel_id=1, source_target_pairs={{0,3},{1,0},{2,1},{3,2},{4,7},{5,4},{6,5},{7,6},{8,11},{9,8},{10,9... | collective-permute-start | bytes 1179656 | tf_op jit(solution)/shard_map/ppermute | solution.py:205
  66.5 39.1 %collective-permute-start.5 = (bf16[256,768]{1,0:T(8,128)(2,1)}, bf16[256,768]{1,0:T(8,128)(2,1)S(1)}, u32[]{:S(2)}, u32[]{:S(2)}) collective-permute-start(bf16[256,768]{1,0:T(8,128)(2,1)} %shard_map.68.own_ref), channel_id=1, source_target_pairs={{0,2},{1,3},{2,0},{3,1},{4,6},{5,7},{6,4},{7,5},{8,10},{9,11},{10,... | collective-permute-start | bytes 1179656 | tf_op jit(solution)/shard_map/ppermute | solution.py:205
  69.0 36.7 %collective-permute-start.4 = (bf16[256,768]{1,0:T(8,128)(2,1)}, bf16[256,768]{1,0:T(8,128)(2,1)S(1)}, u32[]{:S(2)}, u32[]{:S(2)}) collective-permute-start(bf16[256,768]{1,0:T(8,128)(2,1)} %shard_map.68.own_ref), channel_id=1, source_target_pairs={{0,1},{1,2},{2,3},{3,0},{4,5},{5,6},{6,7},{7,4},{8,9},{9,10},{10,1... | collective-permute-start | bytes 1179656 | tf_op jit(solution)/shard_map/ppermute | solution.py:205
  89.2 1.0 copy-start.2
  92.6 23.5 %collective-permute-start.3 = (bf16[256,768]{1,0:T(8,128)(2,1)}, bf16[256,768]{1,0:T(8,128)(2,1)S(1)}, u32[]{:S(2)}, u32[]{:S(2)}) collective-permute-start(bf16[256,768]{1,0:T(8,128)(2,1)} %shard_map.66.own_ref), channel_id=1, source_target_pairs={{0,3},{1,0},{2,1},{3,2},{4,7},{5,4},{6,5},{7,6},{8,11},{9,8},{10,9... | collective-permute-start | bytes 1179656 | tf_op jit(solution)/shard_map/ppermute | solution.py:205
  99.4 16.7 %collective-permute-start.2 = (bf16[256,768]{1,0:T(8,128)(2,1)}, bf16[256,768]{1,0:T(8,128)(2,1)S(1)}, u32[]{:S(2)}, u32[]{:S(2)}) collective-permute-start(bf16[256,768]{1,0:T(8,128)(2,1)} %shard_map.66.own_ref), channel_id=1, source_target_pairs={{0,2},{1,3},{2,0},{3,1},{4,6},{5,7},{6,4},{7,5},{8,10},{9,11},{10,... | collective-permute-start | bytes 1179656 | tf_op jit(solution)/shard_map/ppermute | solution.py:205
  101.6 4.1 %copy-start.3 = (bf16[256,768]{1,0:T(8,128)(2,1)}, bf16[256,768]{1,0:T(8,128)(2,1)S(1)}, u32[]{:S(2)}) copy-start(bf16[256,768]{1,0:T(8,128)(2,1)S(1)} %collective-permute-done.6.three_ref) | copy-start | bytes 1179652
  101.6 20.9 %collective-permute-start.1 = (bf16[256,768]{1,0:T(8,128)(2,1)}, bf16[256,768]{1,0:T(8,128)(2,1)S(1)}, u32[]{:S(2)}, u32[]{:S(2)}) collective-permute-start(bf16[256,768]{1,0:T(8,128)(2,1)} %shard_map.66.own_ref), channel_id=1, source_target_pairs={{0,1},{1,2},{2,3},{3,0},{4,5},{5,6},{6,7},{7,4},{8,9},{9,10},{10,1... | collective-permute-start | bytes 1179656 | tf_op jit(solution)/shard_map/ppermute | solution.py:205
  105.7 0.8 copy-start.4
  105.7 0.9 copy-start.5
  116.1 6.4 %copy-start.6 = (bf16[256,768]{1,0:T(8,128)(2,1)}, bf16[256,768]{1,0:T(8,128)(2,1)S(1)}, u32[]{:S(2)}) copy-start(bf16[256,768]{1,0:T(8,128)(2,1)S(1)} %collective-permute-done.3.three_ref) | copy-start | bytes 1179652
  116.1 6.4 %copy-start.7 = (bf16[256,768]{1,0:T(8,128)(2,1)}, bf16[256,768]{1,0:T(8,128)(2,1)S(1)}, u32[]{:S(2)}) copy-start(bf16[256,768]{1,0:T(8,128)(2,1)S(1)} %collective-permute-done.2.two_ref) | copy-start | bytes 1179652
  122.5 0.8 copy-start.8
Sparse Core Ops, SparseCore 0:
  24.5 58.1 all-gather.2

commit v4 on v3

--- a/solution.py
+++ b/solution.py
@@ -99,17 +99,17 @@
             pl.BlockSpec(gain.shape, lambda i: (0, 0)),
         ],
         out_specs=pl.BlockSpec((owners * tok, width), lambda i: (0, 0)),
-        cost_estimate=pl.CostEstimate(flops=50_625_000_000, bytes_accessed=0, transcendentals=0),
-        compiler_params=pltpu.CompilerParams(vmem_limit_bytes=VMEM_LIMIT),
+        cost_estimate=pl.CostEstimate(flops=50500000000, bytes_accessed=0, transcendentals=0),
+        compiler_params=pltpu.CompilerParams(vmem_limit_bytes=16 * 1024 * 1024),
     )(sel, rows, gain)
 
 
 def project_kernel(width, place_ref, own_ref, one_ref, two_ref, three_ref, w_ref, inv_ref, *rest):
     out_ref, scale_ref = rest[-2:]
     blocks = (own_ref, one_ref, two_ref, three_ref)
-    half = pl.program_id(0)
-
-    @pl.when(half == 0)
+    half = lax.div(pl.program_id(0), 2)
+
+    @pl.when(pl.program_id(0) == 0)
     def _():
         total = jnp.zeros(scale_ref.shape, F32)
         for k, block in enumerate(blocks):
@@ -133,7 +133,7 @@
     shards, halves, share, columns = weight.shape
     whole = pl.BlockSpec((rows, quarter), lambda j, p: (0, 0))
     in_specs = [whole] * 4 + [
-        pl.BlockSpec((shards, 1, share, columns), lambda j, p: (0, j, 0, 0)),
+        pl.BlockSpec((shards, 1, share, columns // 2), lambda j, p: (0, j // 2, 0, j % 2)),
         pl.BlockSpec(inv_gain.shape, lambda j, p: (0, 0, 0)),
     ]
     args = [place, *blocks, weight, inv_gain]
@@ -147,13 +147,13 @@
         out_shape=jax.ShapeDtypeStruct((total_rows, halves * columns), BF16),
         grid_spec=pltpu.PrefetchScalarGridSpec(
             num_scalar_prefetch=1,
-            grid=(halves,),
+            grid=(2 * halves,),
             in_specs=in_specs,
-            out_specs=pl.BlockSpec((rows, columns), lambda j, p: (row_block, j)),
+            out_specs=pl.BlockSpec((rows, columns // 2), lambda j, p: (row_block, j)),
             scratch_shapes=[pltpu.VMEM((rows, 1), F32)],
         ),
         input_output_aliases=aliases,
-        compiler_params=pltpu.CompilerParams(vmem_limit_bytes=VMEM_LIMIT),
+        compiler_params=pltpu.CompilerParams(vmem_limit_bytes=24 * 1024 * 1024),
     )(*args)
 
 

time: 137 us -> 132 us (0.964)
  the two profiles are of different devices: /device:TPU:321 before, /device:TPU:449 now
where the time goes in v4:
time: 132 us
  waiting for transfers between devices  42.2 us (32%)
  starting transfers between devices  33.3 us (25%)
  Pallas kernels  25 us (19%)
  between operations  13.6 us (10%)
  blocking collectives  9.14 us (7%)
  local copies, waits for them, and re-layouts  7.7 us (6%)
    all_to_all x2, waiting for transfers between devices, local(): arrived = lax.all_to_all(packed, 'expert', 0, 0, tiled=True)  27.7 us
    ppermute x6, starting transfers between devices, local(): lax.ppermute(own, 'tensor', [(i, (i + k) % tensors) for i in range(tensor...  18.7 us
    pallas_call x2, Pallas kernels, project(): pl.pallas_call(functools.partial(project_kernel, 4 * quarter), out_shape=...  11.4 us
    pallas_call x2, Pallas kernels, pack(): pl.pallas_call(functools.partial(pack_kernel, owners // experts, first),...  9.48 us
    all_gather x1, blocking collectives, local(): ids = lax.all_gather(ids, 'tensor')  9.14 us
    ppermute x6, waiting for transfers between devices, local(): lax.ppermute(own, 'tensor', [(i, (i + k) % tensors) for i in range(tensor...  8.01 us
    all_to_all x2, starting transfers between devices, local(): arrived = lax.all_to_all(packed, 'expert', 0, 0, tiled=True)  7.97 us
    unnamed x18, local copies, waits for them, and re-layouts  6.72 us
  transfers between devices with their start and end apart: 10, of which 4 were waited for; matrix products, arithmetic and copies ran while one was open for 1% of the time, Pallas kernels for 15%

profile of v4, /device:TPU:449, one launch (start us, length us, event | category | flops | bytes accessed | tf_op | source)
XLA Modules:
  0.0 131.7 jit_solution(438512774471900913)
XLA Ops:
  6.5 0.0 copy-start
  6.5 1.1 copy-done
  7.7 6.7 %collective-permute-start = (bf16[384,512]{1,0:T(8,128)(2,1)S(1)}, bf16[384,512]{1,0:T(8,128)(2,1)S(1)}, u32[]{:S(2)}, u32[]{:S(2)}) collective-permute-start(bf16[384,512]{1,0:T(8,128)(2,1)S(1)} %constant_dynamic-slice_fusion), channel_id=1, source_target_pairs={{0,0},{4,4},{8,8},{12,12},{16,16},{20,20},{24,24},{28,28},{48,32},... | collective-permute-start | bytes 1179656 | tf_op jit(solution)/shard_map/ppermute | solution.py:178
  14.4 4.7 %shard_map.67 = bf16[8,2,48,768]{3,2,1,0:T(8,128)(2,1)} custom-call(s32[12]{0:T(128)} %bitcast.13, bf16[48,32,768]{2,1,0:T(8,128)(2,1)} %bitcast.10), custom_call_target="tpu_custom_call" | custom-call | tf_op jit(solution)/shard_map/pallas_call | solution.py:38
  19.0 0.0 copy-start.7
  19.0 0.0 copy-start.8
  19.0 3.7 %all-to-all-start.1 = ((bf16[8,2,48,768]{3,2,1,0:T(8,128)(2,1)}), bf16[8,2,48,768]{3,2,1,0:T(8,128)(2,1)S(1)}, u32[]{:S(2)}, u32[]{:S(2)}) async-start(bf16[8,2,48,768]{3,2,1,0:T(8,128)(2,1)} %shard_map.67), calls=%async_computation.1 | async-start | bytes 2359296 | tf_op jit(solution)/shard_map/all_to_all | solution.py:202
  22.7 0.0 all-gather.3.cloned.1.call-start
  22.8 0.0 copy-done.7
  22.8 0.0 copy-done.8
  22.8 6.4 %collective-permute-done = bf16[384,512]{1,0:T(8,128)(2,1)S(1)} collective-permute-done((bf16[384,512]{1,0:T(8,128)(2,1)S(1)}, bf16[384,512]{1,0:T(8,128)(2,1)S(1)}, u32[]{:S(2)}, u32[]{:S(2)}) %collective-permute-start) | collective-permute-done | bytes 393248 | tf_op jit(solution)/shard_map/ppermute | solution.py:178
  29.2 0.0 copy-start.5
  29.2 0.8 copy-done.5
  30.0 0.0 all-gather.3.cloned.1.call-update
  30.1 0.0 copy-start.6
  30.1 4.8 %shard_map.65 = bf16[8,2,48,768]{3,2,1,0:T(8,128)(2,1)} custom-call(s32[12]{0:T(128)} %bitcast.14, bf16[48,32,768]{2,1,0:T(8,128)(2,1)} %bitcast.11), custom_call_target="tpu_custom_call" | custom-call | tf_op jit(solution)/shard_map/pallas_call | solution.py:38
  34.9 0.0 copy-done.6
  34.9 0.1 dynamic_slice.7
  35.0 9.1 %all-gather = s32[512,4]{0,1:T(4,128)S(1)} all-gather(s32[128,4]{0,1:T(4,128)S(1)} %pad_add_fusion), channel_id=2, replica_groups=mesh['dp'=16,'expert'=8,'tensor'=4] {'tensor'}, dimensions={0}, use_global_device_ids=true | all-gather | bytes 10240 | tf_op jit(solution)/shard_map/all_gather | solution.py:186
  44.1 0.9 copy.8
  45.0 3.5 %shard_map.64.sel_ref = bf16[4,128,384]{2,1,0:T(8,128)(2,1)} custom-call(s32[4,128,4]{2,1,0:T(8,128)} %bitcast.12), custom_call_target="tpu_custom_call" | custom-call | tf_op jit(solution)/shard_map/pallas_call | solution.py:74
  48.4 6.3 %all-to-all-done.1.rows_ref = bf16[8,2,48,768]{3,2,1,0:T(8,128)(2,1)S(1)} async-done(((bf16[8,2,48,768]{3,2,1,0:T(8,128)(2,1)}), bf16[8,2,48,768]{3,2,1,0:T(8,128)(2,1)S(1)}, u32[]{:S(2)}, u32[]{:S(2)}) %all-to-all-start.1) | async-done | bytes 1179680 | tf_op jit(solution)/shard_map/all_to_all | solution.py:202
  54.7 4.3 %all-to-all-start = ((bf16[8,2,48,768]{3,2,1,0:T(8,128)(2,1)}), bf16[8,2,48,768]{3,2,1,0:T(8,128)(2,1)S(1)}, u32[]{:S(2)}, u32[]{:S(2)}) async-start(bf16[8,2,48,768]{3,2,1,0:T(8,128)(2,1)} %shard_map.65), calls=%async_computation | async-start | bytes 2359296 | tf_op jit(solution)/shard_map/all_to_all | solution.py:202
  59.0 0.0 copy-start.3
  59.0 1.0 copy-done.3
  60.0 0.4 shard_map.68.own_ref
  60.4 4.4 %collective-permute-start.6 = (bf16[256,768]{1,0:T(8,128)(2,1)S(1)}, bf16[256,768]{1,0:T(8,128)(2,1)S(1)}, u32[]{:S(2)}, u32[]{:S(2)}) collective-permute-start(bf16[256,768]{1,0:T(8,128)(2,1)S(1)} %shard_map.68.own_ref), channel_id=1, source_target_pairs={{0,3},{1,0},{2,1},{3,2},{4,7},{5,4},{6,5},{7,6},{8,11},{9,8},{10,9... | collective-permute-start | bytes 1179656 | tf_op jit(solution)/shard_map/ppermute | solution.py:205
  64.8 2.4 %collective-permute-start.5 = (bf16[256,768]{1,0:T(8,128)(2,1)S(1)}, bf16[256,768]{1,0:T(8,128)(2,1)S(1)}, u32[]{:S(2)}, u32[]{:S(2)}) collective-permute-start(bf16[256,768]{1,0:T(8,128)(2,1)S(1)} %shard_map.68.own_ref), channel_id=1, source_target_pairs={{0,2},{1,3},{2,0},{3,1},{4,6},{5,7},{6,4},{7,5},{8,10},{9,11},{10,... | collective-permute-start | bytes 1179656 | tf_op jit(solution)/shard_map/ppermute | solution.py:205
  67.2 2.5 %collective-permute-start.4 = (bf16[256,768]{1,0:T(8,128)(2,1)S(1)}, bf16[256,768]{1,0:T(8,128)(2,1)}, u32[]{:S(2)}, u32[]{:S(2)}) collective-permute-start(bf16[256,768]{1,0:T(8,128)(2,1)S(1)} %shard_map.68.own_ref), channel_id=1, source_target_pairs={{0,1},{1,2},{2,3},{3,0},{4,5},{5,6},{6,7},{7,4},{8,9},{9,10},{10,1... | collective-permute-start | bytes 1179656 | tf_op jit(solution)/shard_map/ppermute | solution.py:205
  69.7 21.4 %all-to-all-done.rows_ref = bf16[8,2,48,768]{3,2,1,0:T(8,128)(2,1)S(1)} async-done(((bf16[8,2,48,768]{3,2,1,0:T(8,128)(2,1)}), bf16[8,2,48,768]{3,2,1,0:T(8,128)(2,1)S(1)}, u32[]{:S(2)}, u32[]{:S(2)}) %all-to-all-start) | async-done | bytes 1179680 | tf_op jit(solution)/shard_map/all_to_all | solution.py:202
  91.1 0.0 copy-start.4
  91.2 1.0 copy-done.4
  92.1 0.4 shard_map.66.own_ref
  92.5 4.4 %collective-permute-start.3 = (bf16[256,768]{1,0:T(8,128)(2,1)S(1)}, bf16[256,768]{1,0:T(8,128)(2,1)S(1)}, u32[]{:S(2)}, u32[]{:S(2)}) collective-permute-start(bf16[256,768]{1,0:T(8,128)(2,1)S(1)} %shard_map.66.own_ref), channel_id=1, source_target_pairs={{0,3},{1,0},{2,1},{3,2},{4,7},{5,4},{6,5},{7,6},{8,11},{9,8},{10,9... | collective-permute-start | bytes 1179656 | tf_op jit(solution)/shard_map/ppermute | solution.py:205
  96.9 2.4 %collective-permute-start.2 = (bf16[256,768]{1,0:T(8,128)(2,1)S(1)}, bf16[256,768]{1,0:T(8,128)(2,1)S(1)}, u32[]{:S(2)}, u32[]{:S(2)}) collective-permute-start(bf16[256,768]{1,0:T(8,128)(2,1)S(1)} %shard_map.66.own_ref), channel_id=1, source_target_pairs={{0,2},{1,3},{2,0},{3,1},{4,6},{5,7},{6,4},{7,5},{8,10},{9,11},{10,... | collective-permute-start | bytes 1179656 | tf_op jit(solution)/shard_map/ppermute | solution.py:205
  99.4 0.0 collective-permute-done.6.three_ref
  99.4 2.5 %collective-permute-start.1 = (bf16[256,768]{1,0:T(8,128)(2,1)S(1)}, bf16[256,768]{1,0:T(8,128)(2,1)S(1)}, u32[]{:S(2)}, u32[]{:S(2)}) collective-permute-start(bf16[256,768]{1,0:T(8,128)(2,1)S(1)} %shard_map.66.own_ref), channel_id=1, source_target_pairs={{0,1},{1,2},{2,3},{3,0},{4,5},{5,6},{6,7},{7,4},{8,9},{9,10},{10,1... | collective-permute-start | bytes 1179656 | tf_op jit(solution)/shard_map/ppermute | solution.py:205
  101.9 0.1 pad_add_fusion.1.place_ref
  102.0 0.7 broadcast_divide_fusion
  102.7 0.0 collective-permute-done.5.two_ref
  102.7 0.0 collective-permute-done.4.one_ref
  102.7 0.0 all-gather.3.cloned.1.call-done
  102.7 0.0 copy-start.1
  102.7 2.8 %copy-done.1 = bf16[6144,512]{1,0:T(8,128)(2,1)S(1)} copy-done((bf16[6144,512]{1,0:T(8,128)(2,1)S(1)}, bf16[6144,512]{1,0:T(8,128)(2,1)}, u32[]{:S(2)}) %copy-start.1) | copy-done | bytes 6291480
  105.5 0.0 copy-start.2
  105.5 6.3 %shard_map.69.rest_0_ = bf16[512,1024]{1,0:T(8,128)(2,1)} custom-call(s32[5]{0:T(128)S(1)} %pad_add_fusion.1.place_ref, bf16[256,768]{1,0:T(8,128)(2,1)S(1)} %shard_map.68.own_ref, bf16[256,768]{1,0:T(8,128)(2,1)} %collective-permute-done.4.one_ref, bf16[256,768]{1,0:T(8,128)(2,1)S(1)} %collective-permute-done.5.two_ref, ...), custom_call_target="tpu_custom_call" | custom-call | tf_op jit(solution)/shard_map/pallas_call | solution.py:145
  111.8 0.0 collective-permute-done.3.three_ref
  111.8 0.0 collective-permute-done.2.two_ref
  111.8 8.0 %collective-permute-done.1.one_ref = bf16[256,768]{1,0:T(8,128)(2,1)S(1)} collective-permute-done((bf16[256,768]{1,0:T(8,128)(2,1)S(1)}, bf16[256,768]{1,0:T(8,128)(2,1)S(1)}, u32[]{:S(2)}, u32[]{:S(2)}) %collective-permute-start.1) | collective-permute-done | bytes 393248 | tf_op jit(solution)/shard_map/ppermute | solution.py:205
  119.8 0.0 copy-done.2
  119.8 5.1 %shard_map.70 = bf16[512,1024]{1,0:T(8,128)(2,1)} custom-call(s32[5]{0:T(128)S(1)} %pad_add_fusion.1.place_ref, bf16[256,768]{1,0:T(8,128)(2,1)S(1)} %shard_map.66.own_ref, bf16[256,768]{1,0:T(8,128)(2,1)S(1)} %collective-permute-done.1.one_ref, bf16[256,768]{1,0:T(8,128)(2,1)S(1)} %collective-permute-done.2.two_ref, ...), custom_call_target="tpu_custom_call", output_to_operand_aliasing={{}: (7, {})} | custom-call | tf_op jit(solution)/shard_map/pallas_call | solution.py:145
  (4 shorter events, 0.1 us)
Async XLA Ops:
  6.5 1.1 copy-start
  7.7 21.5 %collective-permute-start = (bf16[384,512]{1,0:T(8,128)(2,1)S(1)}, bf16[384,512]{1,0:T(8,128)(2,1)S(1)}, u32[]{:S(2)}, u32[]{:S(2)}) collective-permute-start(bf16[384,512]{1,0:T(8,128)(2,1)S(1)} %constant_dynamic-slice_fusion), channel_id=1, source_target_pairs={{0,0},{4,4},{8,8},{12,12},{16,16},{20,20},{24,24},{28,28},{48,32},... | collective-permute-start | bytes 1179656 | tf_op jit(solution)/shard_map/ppermute | solution.py:178
  19.0 3.8 %copy-start.7 = (s32[128,2]{0,1:T(2,128)S(1)}, s32[128,2]{0,1:T(2,128)}, u32[]{:S(2)}) copy-start(s32[128,2]{0,1:T(2,128)} %param.9) | copy-start | bytes 3076
  19.0 3.8 %copy-start.8 = (s32[128,2]{0,1:T(2,128)S(1)}, s32[128,2]{0,1:T(2,128)}, u32[]{:S(2)}) copy-start(s32[128,2]{0,1:T(2,128)} %param.8) | copy-start | bytes 3076
  19.0 35.7 %all-to-all-start.1 = ((bf16[8,2,48,768]{3,2,1,0:T(8,128)(2,1)}), bf16[8,2,48,768]{3,2,1,0:T(8,128)(2,1)S(1)}, u32[]{:S(2)}, u32[]{:S(2)}) async-start(bf16[8,2,48,768]{3,2,1,0:T(8,128)(2,1)} %shard_map.67), calls=%async_computation.1 | async-start | bytes 2359296 | tf_op jit(solution)/shard_map/all_to_all | solution.py:202
  22.7 80.0 %all-gather.3.cloned.1.call-start = ((), (), s32[]{:S(2)}) async-start(), calls=%async_computation.2 | async-start | bytes 6684672 | tf_op jit(solution)/shard_map/all_gather | solution.py:187
  29.2 0.8 copy-start.5
  30.1 4.8 %copy-start.6 = (bf16[3072]{0:T(1024)(128)(2,1)S(1)}, bf16[3072]{0:T(1024)(128)(2,1)}, u32[]{:S(2)}) copy-start(bf16[3072]{0:T(1024)(128)(2,1)} %param.10) | copy-start | bytes 18436
  54.7 36.4 %all-to-all-start = ((bf16[8,2,48,768]{3,2,1,0:T(8,128)(2,1)}), bf16[8,2,48,768]{3,2,1,0:T(8,128)(2,1)S(1)}, u32[]{:S(2)}, u32[]{:S(2)}) async-start(bf16[8,2,48,768]{3,2,1,0:T(8,128)(2,1)} %shard_map.65), calls=%async_computation | async-start | bytes 2359296 | tf_op jit(solution)/shard_map/all_to_all | solution.py:202
  59.0 1.0 copy-start.3
  60.4 39.0 %collective-permute-start.6 = (bf16[256,768]{1,0:T(8,128)(2,1)S(1)}, bf16[256,768]{1,0:T(8,128)(2,1)S(1)}, u32[]{:S(2)}, u32[]{:S(2)}) collective-permute-start(bf16[256,768]{1,0:T(8,128)(2,1)S(1)} %shard_map.68.own_ref), channel_id=1, source_target_pairs={{0,3},{1,0},{2,1},{3,2},{4,7},{5,4},{6,5},{7,6},{8,11},{9,8},{10,9... | collective-permute-start | bytes 1179656 | tf_op jit(solution)/shard_map/ppermute | solution.py:205
  64.8 37.9 %collective-permute-start.5 = (bf16[256,768]{1,0:T(8,128)(2,1)S(1)}, bf16[256,768]{1,0:T(8,128)(2,1)S(1)}, u32[]{:S(2)}, u32[]{:S(2)}) collective-permute-start(bf16[256,768]{1,0:T(8,128)(2,1)S(1)} %shard_map.68.own_ref), channel_id=1, source_target_pairs={{0,2},{1,3},{2,0},{3,1},{4,6},{5,7},{6,4},{7,5},{8,10},{9,11},{10,... | collective-permute-start | bytes 1179656 | tf_op jit(solution)/shard_map/ppermute | solution.py:205
  67.2 35.5 %collective-permute-start.4 = (bf16[256,768]{1,0:T(8,128)(2,1)S(1)}, bf16[256,768]{1,0:T(8,128)(2,1)}, u32[]{:S(2)}, u32[]{:S(2)}) collective-permute-start(bf16[256,768]{1,0:T(8,128)(2,1)S(1)} %shard_map.68.own_ref), channel_id=1, source_target_pairs={{0,1},{1,2},{2,3},{3,0},{4,5},{5,6},{6,7},{7,4},{8,9},{9,10},{10,1... | collective-permute-start | bytes 1179656 | tf_op jit(solution)/shard_map/ppermute | solution.py:205
  91.1 1.0 copy-start.4
  92.5 19.3 %collective-permute-start.3 = (bf16[256,768]{1,0:T(8,128)(2,1)S(1)}, bf16[256,768]{1,0:T(8,128)(2,1)S(1)}, u32[]{:S(2)}, u32[]{:S(2)}) collective-permute-start(bf16[256,768]{1,0:T(8,128)(2,1)S(1)} %shard_map.66.own_ref), channel_id=1, source_target_pairs={{0,3},{1,0},{2,1},{3,2},{4,7},{5,4},{6,5},{7,6},{8,11},{9,8},{10,9... | collective-permute-start | bytes 1179656 | tf_op jit(solution)/shard_map/ppermute | solution.py:205
  96.9 14.9 %collective-permute-start.2 = (bf16[256,768]{1,0:T(8,128)(2,1)S(1)}, bf16[256,768]{1,0:T(8,128)(2,1)S(1)}, u32[]{:S(2)}, u32[]{:S(2)}) collective-permute-start(bf16[256,768]{1,0:T(8,128)(2,1)S(1)} %shard_map.66.own_ref), channel_id=1, source_target_pairs={{0,2},{1,3},{2,0},{3,1},{4,6},{5,7},{6,4},{7,5},{8,10},{9,11},{10,... | collective-permute-start | bytes 1179656 | tf_op jit(solution)/shard_map/ppermute | solution.py:205
  99.4 20.4 %collective-permute-start.1 = (bf16[256,768]{1,0:T(8,128)(2,1)S(1)}, bf16[256,768]{1,0:T(8,128)(2,1)S(1)}, u32[]{:S(2)}, u32[]{:S(2)}) collective-permute-start(bf16[256,768]{1,0:T(8,128)(2,1)S(1)} %shard_map.66.own_ref), channel_id=1, source_target_pairs={{0,1},{1,2},{2,3},{3,0},{4,5},{5,6},{6,7},{7,4},{8,9},{9,10},{10,1... | collective-permute-start | bytes 1179656 | tf_op jit(solution)/shard_map/ppermute | solution.py:205
  102.7 2.8 %copy-start.1 = (bf16[6144,512]{1,0:T(8,128)(2,1)S(1)}, bf16[6144,512]{1,0:T(8,128)(2,1)}, u32[]{:S(2)}) copy-start(bf16[6144,512]{1,0:T(8,128)(2,1)} %all-gather.3.cloned.1.call-done) | copy-start | bytes 18874372
  105.5 14.3 %copy-start.2 = (bf16[6144,512]{1,0:T(8,128)(2,1)S(1)}, bf16[6144,512]{1,0:T(8,128)(2,1)}, u32[]{:S(2)}) copy-start(bf16[6144,512]{1,0:T(8,128)(2,1)} %all-gather.3.cloned.1.call-done) | copy-start | bytes 18874372
Sparse Core Ops, SparseCore 0:
  30.2 51.4 all-gather.2

commit v5 on v4

--- a/solution.py
+++ b/solution.py
@@ -74,6 +74,7 @@
     return pl.pallas_call(
         functools.partial(select_kernel, experts, slots),
         out_shape=jax.ShapeDtypeStruct((owners, tok, experts * slots), BF16),
+        compiler_params=pltpu.CompilerParams(vmem_limit_bytes=16 * 1024 * 1024),
     )(ids)
 
 
@@ -104,9 +105,9 @@
     )(sel, rows, gain)
 
 
-def project_kernel(width, place_ref, own_ref, one_ref, two_ref, three_ref, w_ref, inv_ref, *rest):
+def project_kernel(width, place_ref, own_ref, two_ref, one_ref, three_ref, w_ref, inv_ref, *rest):
     out_ref, scale_ref = rest[-2:]
-    blocks = (own_ref, one_ref, two_ref, three_ref)
+    blocks = (own_ref, two_ref, one_ref, three_ref)
     half = lax.div(pl.program_id(0), 2)
 
     @pl.when(pl.program_id(0) == 0)
@@ -192,7 +193,7 @@
     inv_gain = (1.0 / gain).reshape(tensors, 1, quarter)
     own_gain = lax.dynamic_slice(gain, (quarter_of * quarter,), (quarter,)).reshape(1, quarter)
     place = jnp.concatenate(
-        [mine[None], (quarter_of - jnp.arange(tensors, dtype=jnp.int32)) % tensors]
+        [mine[None], (quarter_of - jnp.array([0, 2, 1, 3], dtype=jnp.int32)) % tensors]
     ).astype(jnp.int32)
 
     out = None
@@ -201,10 +202,11 @@
         n = packed.shape[1]
         arrived = lax.all_to_all(packed, "expert", 0, 0, tiled=True)
         own = combine(sel, first, arrived, own_gain)
-        blocks = [own] + [
-            lax.ppermute(own, "tensor", [(i, (i + k) % tensors) for i in range(tensors)])
-            for k in range(1, tensors)
-        ]
+        sent = {
+            k: lax.ppermute(own, "tensor", [(i, (i + k) % tensors) for i in range(tensors)])
+            for k in (2, 1, 3)
+        }
+        blocks = [own, sent[2], sent[1], sent[3]]
         out = project(place, blocks, weight, inv_gain, tensors * tok, first // n, out)
         first += n
     return out

time: 132 us -> 132 us (level)
  the two profiles are of different devices: /device:TPU:449 before, /device:TPU:321 now
where the time goes in v5:
time: 132 us; the launch traced here: 130 us
  waiting for transfers between devices  42.7 us (32%)
  starting transfers between devices  32.6 us (25%)
  Pallas kernels  23.3 us (18%)
  between operations  13.6 us (10%)
  blocking collectives  9.14 us (7%)
  local copies, waits for them, and re-layouts  7.7 us (6%)
    all_to_all x2, waiting for transfers between devices, local(): arrived = lax.all_to_all(packed, 'expert', 0, 0, tiled=True)  37.6 us
    ppermute x6, starting transfers between devices, local(): lax.ppermute(own, 'tensor', [(i, (i + k) % tensors) for i in range(tensor...  19.9 us
    pallas_call x2, Pallas kernels, project(): pl.pallas_call(functools.partial(project_kernel, 4 * quarter), out_shape=...  11.4 us
    pallas_call x2, Pallas kernels, pack(): pl.pallas_call(functools.partial(pack_kernel, owners // experts, first),...  9.45 us
    all_gather x1, blocking collectives, local(): ids = lax.all_gather(ids, 'tensor')  9.14 us
    all_to_all x2, starting transfers between devices, local(): arrived = lax.all_to_all(packed, 'expert', 0, 0, tiled=True)  7.62 us
    unnamed x22, local copies, waits for them, and re-layouts  7.44 us
    ppermute x1, starting transfers between devices, local(): w = lax.ppermute(w, ('dp', 'expert'), fetch)  5.1 us
  transfers between devices with their start and end apart: 10, of which 3 were waited for; matrix products, arithmetic and copies ran while one was open for 1% of the time, Pallas kernels for 14%

profile of v5, /device:TPU:321, one launch (start us, length us, event | category | flops | bytes accessed | tf_op | source)
XLA Modules:
  0.0 129.9 jit_solution(11024358847052834438)
XLA Ops:
  6.5 0.0 copy-start
  6.5 1.1 copy-done
  7.7 5.1 %collective-permute-start = (bf16[384,512]{1,0:T(8,128)(2,1)S(1)}, bf16[384,512]{1,0:T(8,128)(2,1)S(1)}, u32[]{:S(2)}, u32[]{:S(2)}) collective-permute-start(bf16[384,512]{1,0:T(8,128)(2,1)S(1)} %constant_dynamic-slice_fusion), channel_id=1, source_target_pairs={{0,0},{4,4},{8,8},{12,12},{16,16},{20,20},{24,24},{28,28},{48,32},... | collective-permute-start | bytes 1179656 | tf_op jit(solution)/shard_map/ppermute | solution.py:179
  12.8 4.6 %shard_map.76 = bf16[8,2,48,768]{3,2,1,0:T(8,128)(2,1)} custom-call(s32[12]{0:T(128)} %bitcast.13, bf16[48,32,768]{2,1,0:T(8,128)(2,1)} %bitcast.11), custom_call_target="tpu_custom_call" | custom-call | tf_op jit(solution)/shard_map/pallas_call | solution.py:38
  17.5 0.0 copy-start.8
  17.5 0.0 copy-start.9
  17.5 4.0 %all-to-all-start.1 = ((bf16[8,2,48,768]{3,2,1,0:T(8,128)(2,1)}), bf16[8,2,48,768]{3,2,1,0:T(8,128)(2,1)S(1)}, u32[]{:S(2)}, u32[]{:S(2)}) async-start(bf16[8,2,48,768]{3,2,1,0:T(8,128)(2,1)} %shard_map.76), calls=%async_computation.1 | async-start | bytes 2359296 | tf_op jit(solution)/shard_map/all_to_all | solution.py:203
  21.5 0.0 all-gather.3.cloned.1.call-start
  21.5 0.0 copy-done.8
  21.6 0.0 copy-done.9
  21.6 0.0 collective-permute-done
  21.6 0.0 copy-start.6
  21.6 0.8 copy-done.6
  22.4 0.0 all-gather.3.cloned.1.call-update
  22.4 0.0 copy-start.7
  22.4 4.8 %shard_map.74 = bf16[8,2,48,768]{3,2,1,0:T(8,128)(2,1)} custom-call(s32[12]{0:T(128)} %bitcast.14, bf16[48,32,768]{2,1,0:T(8,128)(2,1)} %bitcast.12), custom_call_target="tpu_custom_call" | custom-call | tf_op jit(solution)/shard_map/pallas_call | solution.py:38
  27.2 0.0 copy-done.7
  27.2 0.1 dynamic_slice.7
  27.3 9.1 %all-gather = s32[512,4]{0,1:T(4,128)S(1)} all-gather(s32[128,4]{0,1:T(4,128)S(1)} %pad_add_fusion), channel_id=2, replica_groups=mesh['dp'=16,'expert'=8,'tensor'=4] {'tensor'}, dimensions={0}, use_global_device_ids=true | all-gather | bytes 10240 | tf_op jit(solution)/shard_map/all_gather | solution.py:187
  36.4 0.1 copy.9
  36.6 1.8 %shard_map.73.sel_ref = bf16[4,128,384]{2,1,0:T(8,128)(2,1)S(1)} custom-call(s32[4,128,4]{2,1,0:T(8,128)S(1)} %bitcast.8), custom_call_target="tpu_custom_call" | custom-call | tf_op jit(solution)/shard_map/pallas_call | solution.py:74
  38.4 0.0 copy-start.3
  38.4 0.7 copy-done.3
  39.1 17.0 %all-to-all-done.1.rows_ref = bf16[8,2,48,768]{3,2,1,0:T(8,128)(2,1)S(1)} async-done(((bf16[8,2,48,768]{3,2,1,0:T(8,128)(2,1)}), bf16[8,2,48,768]{3,2,1,0:T(8,128)(2,1)S(1)}, u32[]{:S(2)}, u32[]{:S(2)}) %all-to-all-start.1) | async-done | bytes 1179680 | tf_op jit(solution)/shard_map/all_to_all | solution.py:203
  56.1 3.6 %all-to-all-start = ((bf16[8,2,48,768]{3,2,1,0:T(8,128)(2,1)}), bf16[8,2,48,768]{3,2,1,0:T(8,128)(2,1)S(1)}, u32[]{:S(2)}, u32[]{:S(2)}) async-start(bf16[8,2,48,768]{3,2,1,0:T(8,128)(2,1)} %shard_map.74), calls=%async_computation | async-start | bytes 2359296 | tf_op jit(solution)/shard_map/all_to_all | solution.py:203
  59.7 0.0 copy-start.4
  59.7 1.0 copy-done.4
  60.7 0.0 copy-start.10
  60.7 0.4 shard_map.77.own_ref
  61.1 4.4 %collective-permute-start.6 = (bf16[256,768]{1,0:T(8,128)(2,1)S(1)}, bf16[256,768]{1,0:T(8,128)(2,1)S(1)}, u32[]{:S(2)}, u32[]{:S(2)}) collective-permute-start(bf16[256,768]{1,0:T(8,128)(2,1)S(1)} %shard_map.77.own_ref), channel_id=1, source_target_pairs={{0,3},{1,0},{2,1},{3,2},{4,7},{5,4},{6,5},{7,6},{8,11},{9,8},{10,9... | collective-permute-start | bytes 1179656 | tf_op jit(solution)/shard_map/ppermute | solution.py:206
  65.5 1.9 %collective-permute-start.5 = (bf16[256,768]{1,0:T(8,128)(2,1)S(1)}, bf16[256,768]{1,0:T(8,128)(2,1)S(1)}, u32[]{:S(2)}, u32[]{:S(2)}) collective-permute-start(bf16[256,768]{1,0:T(8,128)(2,1)S(1)} %shard_map.77.own_ref), channel_id=1, source_target_pairs={{0,1},{1,2},{2,3},{3,0},{4,5},{5,6},{6,7},{7,4},{8,9},{9,10},{10,1... | collective-permute-start | bytes 1179656 | tf_op jit(solution)/shard_map/ppermute | solution.py:206
  67.4 3.6 %collective-permute-start.4 = (bf16[256,768]{1,0:T(8,128)(2,1)S(1)}, bf16[256,768]{1,0:T(8,128)(2,1)}, u32[]{:S(2)}, u32[]{:S(2)}) collective-permute-start(bf16[256,768]{1,0:T(8,128)(2,1)S(1)} %shard_map.77.own_ref), channel_id=1, source_target_pairs={{0,2},{1,3},{2,0},{3,1},{4,6},{5,7},{6,4},{7,5},{8,10},{9,11},{10,... | collective-permute-start | bytes 1179656 | tf_op jit(solution)/shard_map/ppermute | solution.py:206
  71.0 20.6 %all-to-all-done.rows_ref = bf16[8,2,48,768]{3,2,1,0:T(8,128)(2,1)S(1)} async-done(((bf16[8,2,48,768]{3,2,1,0:T(8,128)(2,1)}), bf16[8,2,48,768]{3,2,1,0:T(8,128)(2,1)S(1)}, u32[]{:S(2)}, u32[]{:S(2)}) %all-to-all-start) | async-done | bytes 1179680 | tf_op jit(solution)/shard_map/all_to_all | solution.py:203
  91.7 0.0 copy-start.5
  91.7 1.0 copy-done.5
  92.7 0.4 shard_map.75.own_ref
  93.0 4.4 %collective-permute-start.3 = (bf16[256,768]{1,0:T(8,128)(2,1)S(1)}, bf16[256,768]{1,0:T(8,128)(2,1)S(1)}, u32[]{:S(2)}, u32[]{:S(2)}) collective-permute-start(bf16[256,768]{1,0:T(8,128)(2,1)S(1)} %shard_map.75.own_ref), channel_id=1, source_target_pairs={{0,3},{1,0},{2,1},{3,2},{4,7},{5,4},{6,5},{7,6},{8,11},{9,8},{10,9... | collective-permute-start | bytes 1179656 | tf_op jit(solution)/shard_map/ppermute | solution.py:206
  97.4 1.9 %collective-permute-start.2 = (bf16[256,768]{1,0:T(8,128)(2,1)S(1)}, bf16[256,768]{1,0:T(8,128)(2,1)S(1)}, u32[]{:S(2)}, u32[]{:S(2)}) collective-permute-start(bf16[256,768]{1,0:T(8,128)(2,1)S(1)} %shard_map.75.own_ref), channel_id=1, source_target_pairs={{0,1},{1,2},{2,3},{3,0},{4,5},{5,6},{6,7},{7,4},{8,9},{9,10},{10,1... | collective-permute-start | bytes 1179656 | tf_op jit(solution)/shard_map/ppermute | solution.py:206
  99.4 0.0 collective-permute-done.6.three_ref
  99.4 3.6 %collective-permute-start.1 = (bf16[256,768]{1,0:T(8,128)(2,1)S(1)}, bf16[256,768]{1,0:T(8,128)(2,1)S(1)}, u32[]{:S(2)}, u32[]{:S(2)}) collective-permute-start(bf16[256,768]{1,0:T(8,128)(2,1)S(1)} %shard_map.75.own_ref), channel_id=1, source_target_pairs={{0,2},{1,3},{2,0},{3,1},{4,6},{5,7},{6,4},{7,5},{8,10},{9,11},{10,... | collective-permute-start | bytes 1179656 | tf_op jit(solution)/shard_map/ppermute | solution.py:206
  103.0 0.0 copy-done.10
  103.0 0.1 pad_add_fusion.1.place_ref
  103.1 0.7 broadcast_divide_fusion
  103.8 0.0 collective-permute-done.5.one_ref
  103.8 0.0 collective-permute-done.4.two_ref
  103.8 0.0 all-gather.3.cloned.1.call-done
  103.8 0.0 copy-start.1
  103.9 2.8 %copy-done.1 = bf16[6144,512]{1,0:T(8,128)(2,1)S(1)} copy-done((bf16[6144,512]{1,0:T(8,128)(2,1)S(1)}, bf16[6144,512]{1,0:T(8,128)(2,1)}, u32[]{:S(2)}) %copy-start.1) | copy-done | bytes 6291480
  106.6 0.0 copy-start.2
  106.6 6.3 %shard_map.78.rest_0_ = bf16[512,1024]{1,0:T(8,128)(2,1)} custom-call(s32[5]{0:T(128)S(1)} %pad_add_fusion.1.place_ref, bf16[256,768]{1,0:T(8,128)(2,1)S(1)} %shard_map.77.own_ref, bf16[256,768]{1,0:T(8,128)(2,1)} %collective-permute-done.4.two_ref, bf16[256,768]{1,0:T(8,128)(2,1)S(1)} %collective-permute-done.5.one_ref, ...), custom_call_target="tpu_custom_call" | custom-call | tf_op jit(solution)/shard_map/pallas_call | solution.py:146
  112.9 0.0 collective-permute-done.3.three_ref
  112.9 0.0 collective-permute-done.2.one_ref
  112.9 5.0 %collective-permute-done.1.two_ref = bf16[256,768]{1,0:T(8,128)(2,1)S(1)} collective-permute-done((bf16[256,768]{1,0:T(8,128)(2,1)S(1)}, bf16[256,768]{1,0:T(8,128)(2,1)S(1)}, u32[]{:S(2)}, u32[]{:S(2)}) %collective-permute-start.1) | collective-permute-done | bytes 393248 | tf_op jit(solution)/shard_map/ppermute | solution.py:206
  117.9 0.0 copy-done.2
  117.9 5.1 %shard_map.79 = bf16[512,1024]{1,0:T(8,128)(2,1)} custom-call(s32[5]{0:T(128)S(1)} %pad_add_fusion.1.place_ref, bf16[256,768]{1,0:T(8,128)(2,1)S(1)} %shard_map.75.own_ref, bf16[256,768]{1,0:T(8,128)(2,1)S(1)} %collective-permute-done.1.two_ref, bf16[256,768]{1,0:T(8,128)(2,1)S(1)} %collective-permute-done.2.one_ref, ...), custom_call_target="tpu_custom_call", output_to_operand_aliasing={{}: (7, {})} | custom-call | tf_op jit(solution)/shard_map/pallas_call | solution.py:146
  (4 shorter events, 0.1 us)
Async XLA Ops:
  6.5 1.1 copy-start
  7.7 13.9 %collective-permute-start = (bf16[384,512]{1,0:T(8,128)(2,1)S(1)}, bf16[384,512]{1,0:T(8,128)(2,1)S(1)}, u32[]{:S(2)}, u32[]{:S(2)}) collective-permute-start(bf16[384,512]{1,0:T(8,128)(2,1)S(1)} %constant_dynamic-slice_fusion), channel_id=1, source_target_pairs={{0,0},{4,4},{8,8},{12,12},{16,16},{20,20},{24,24},{28,28},{48,32},... | collective-permute-start | bytes 1179656 | tf_op jit(solution)/shard_map/ppermute | solution.py:179
  17.5 4.1 %copy-start.8 = (s32[128,2]{0,1:T(2,128)S(1)}, s32[128,2]{0,1:T(2,128)}, u32[]{:S(2)}) copy-start(s32[128,2]{0,1:T(2,128)} %param.10) | copy-start | bytes 3076
  17.5 4.1 %copy-start.9 = (s32[128,2]{0,1:T(2,128)S(1)}, s32[128,2]{0,1:T(2,128)}, u32[]{:S(2)}) copy-start(s32[128,2]{0,1:T(2,128)} %param.9) | copy-start | bytes 3076
  17.5 38.7 %all-to-all-start.1 = ((bf16[8,2,48,768]{3,2,1,0:T(8,128)(2,1)}), bf16[8,2,48,768]{3,2,1,0:T(8,128)(2,1)S(1)}, u32[]{:S(2)}, u32[]{:S(2)}) async-start(bf16[8,2,48,768]{3,2,1,0:T(8,128)(2,1)} %shard_map.76), calls=%async_computation.1 | async-start | bytes 2359296 | tf_op jit(solution)/shard_map/all_to_all | solution.py:203
  21.5 82.3 %all-gather.3.cloned.1.call-start = ((), (), s32[]{:S(2)}) async-start(), calls=%async_computation.2 | async-start | bytes 6684672 | tf_op jit(solution)/shard_map/all_gather | solution.py:188
  21.6 0.8 copy-start.6
  22.4 4.8 %copy-start.7 = (bf16[3072]{0:T(1024)(128)(2,1)S(1)}, bf16[3072]{0:T(1024)(128)(2,1)}, u32[]{:S(2)}) copy-start(bf16[3072]{0:T(1024)(128)(2,1)} %param.11) | copy-start | bytes 18436
  38.4 0.7 copy-start.3
  56.1 35.5 %all-to-all-start = ((bf16[8,2,48,768]{3,2,1,0:T(8,128)(2,1)}), bf16[8,2,48,768]{3,2,1,0:T(8,128)(2,1)S(1)}, u32[]{:S(2)}, u32[]{:S(2)}) async-start(bf16[8,2,48,768]{3,2,1,0:T(8,128)(2,1)} %shard_map.74), calls=%async_computation | async-start | bytes 2359296 | tf_op jit(solution)/shard_map/all_to_all | solution.py:203
  59.7 1.0 copy-start.4
  60.7 42.3 %copy-start.10 = (s32[4]{0:T(128)S(1)}, s32[4]{0:T(128)}, u32[]{:S(2)}) copy-start(s32[4]{0:T(128)} %constant.52) | copy-start | bytes 52
  61.1 38.3 %collective-permute-start.6 = (bf16[256,768]{1,0:T(8,128)(2,1)S(1)}, bf16[256,768]{1,0:T(8,128)(2,1)S(1)}, u32[]{:S(2)}, u32[]{:S(2)}) collective-permute-start(bf16[256,768]{1,0:T(8,128)(2,1)S(1)} %shard_map.77.own_ref), channel_id=1, source_target_pairs={{0,3},{1,0},{2,1},{3,2},{4,7},{5,4},{6,5},{7,6},{8,11},{9,8},{10,9... | collective-permute-start | bytes 1179656 | tf_op jit(solution)/shard_map/ppermute | solution.py:206
  65.5 38.3 %collective-permute-start.5 = (bf16[256,768]{1,0:T(8,128)(2,1)S(1)}, bf16[256,768]{1,0:T(8,128)(2,1)S(1)}, u32[]{:S(2)}, u32[]{:S(2)}) collective-permute-start(bf16[256,768]{1,0:T(8,128)(2,1)S(1)} %shard_map.77.own_ref), channel_id=1, source_target_pairs={{0,1},{1,2},{2,3},{3,0},{4,5},{5,6},{6,7},{7,4},{8,9},{9,10},{10,1... | collective-permute-start | bytes 1179656 | tf_op jit(solution)/shard_map/ppermute | solution.py:206
  67.4 36.4 %collective-permute-start.4 = (bf16[256,768]{1,0:T(8,128)(2,1)S(1)}, bf16[256,768]{1,0:T(8,128)(2,1)}, u32[]{:S(2)}, u32[]{:S(2)}) collective-permute-start(bf16[256,768]{1,0:T(8,128)(2,1)S(1)} %shard_map.77.own_ref), channel_id=1, source_target_pairs={{0,2},{1,3},{2,0},{3,1},{4,6},{5,7},{6,4},{7,5},{8,10},{9,11},{10,... | collective-permute-start | bytes 1179656 | tf_op jit(solution)/shard_map/ppermute | solution.py:206
  91.7 1.0 copy-start.5
  93.0 19.9 %collective-permute-start.3 = (bf16[256,768]{1,0:T(8,128)(2,1)S(1)}, bf16[256,768]{1,0:T(8,128)(2,1)S(1)}, u32[]{:S(2)}, u32[]{:S(2)}) collective-permute-start(bf16[256,768]{1,0:T(8,128)(2,1)S(1)} %shard_map.75.own_ref), channel_id=1, source_target_pairs={{0,3},{1,0},{2,1},{3,2},{4,7},{5,4},{6,5},{7,6},{8,11},{9,8},{10,9... | collective-permute-start | bytes 1179656 | tf_op jit(solution)/shard_map/ppermute | solution.py:206
  97.4 15.5 %collective-permute-start.2 = (bf16[256,768]{1,0:T(8,128)(2,1)S(1)}, bf16[256,768]{1,0:T(8,128)(2,1)S(1)}, u32[]{:S(2)}, u32[]{:S(2)}) collective-permute-start(bf16[256,768]{1,0:T(8,128)(2,1)S(1)} %shard_map.75.own_ref), channel_id=1, source_target_pairs={{0,1},{1,2},{2,3},{3,0},{4,5},{5,6},{6,7},{7,4},{8,9},{9,10},{10,1... | collective-permute-start | bytes 1179656 | tf_op jit(solution)/shard_map/ppermute | solution.py:206
  99.4 18.6 %collective-permute-start.1 = (bf16[256,768]{1,0:T(8,128)(2,1)S(1)}, bf16[256,768]{1,0:T(8,128)(2,1)S(1)}, u32[]{:S(2)}, u32[]{:S(2)}) collective-permute-start(bf16[256,768]{1,0:T(8,128)(2,1)S(1)} %shard_map.75.own_ref), channel_id=1, source_target_pairs={{0,2},{1,3},{2,0},{3,1},{4,6},{5,7},{6,4},{7,5},{8,10},{9,11},{10,... | collective-permute-start | bytes 1179656 | tf_op jit(solution)/shard_map/ppermute | solution.py:206
  103.8 2.8 %copy-start.1 = (bf16[6144,512]{1,0:T(8,128)(2,1)S(1)}, bf16[6144,512]{1,0:T(8,128)(2,1)}, u32[]{:S(2)}) copy-start(bf16[6144,512]{1,0:T(8,128)(2,1)} %all-gather.3.cloned.1.call-done) | copy-start | bytes 18874372
  106.6 11.3 %copy-start.2 = (bf16[6144,512]{1,0:T(8,128)(2,1)S(1)}, bf16[6144,512]{1,0:T(8,128)(2,1)}, u32[]{:S(2)}) copy-start(bf16[6144,512]{1,0:T(8,128)(2,1)} %all-gather.3.cloned.1.call-done) | copy-start | bytes 18874372
Sparse Core Ops, SparseCore 0:
  24.5 58.2 all-gather.2
